TPU v7x, 256 devices: a whole 4x4x8 slice. The times are simulated.
256 devices in a mesh: dp: 16 (over x, z_hi), expert: 16 (over y, z_lo, core).
Axes of the slice: x: 4, y: 4, z: 8 (z_hi: 4, z_lo: 2; z = z_hi * 2 + z_lo), core: 2. Of those that a mesh axis runs over, the one named last changes fastest.
Arguments:
- tokens: bfloat16 [65536, 2048], P(('dp', 'expert')), may hold values from -6 to 6
- cotangent: bfloat16 [65536, 2048], P(('dp', 'expert')), may hold values from -6 to 6
- route_ids: int32 [65536, 8], P(('dp', 'expert')), may hold values from 0 to 127, all different within a row
- route_weights: bfloat16 [65536, 8], P(('dp', 'expert')), may hold values from 0.25 to 1
- capacity: int32 [16], replicated, may hold values from 18 to 24, as said below
- old_owner: int32 [16], replicated, may hold values from 0 to 15, each once
- new_owner: int32 [16], replicated, may hold values from 0 to 15, each once
- w_gate: bfloat16 [16, 2048, 768], P('expert'), may hold values from -0.125 to 0.125
- w_up: bfloat16 [16, 2048, 768], P('expert'), may hold values from -0.125 to 0.125
- w_down: bfloat16 [16, 2048, 768], P('expert'), may hold values from -0.21875 to 0.21875
Outputs:
- grad_x: bfloat16 [65536, 2048], P(('dp', 'expert'))
- grad_weights: bfloat16 [65536, 8], P(('dp', 'expert'))
- grad_gate: bfloat16 [16, 2048, 768], P('expert', 'dp')
- grad_up: bfloat16 [16, 2048, 768], P('expert', 'dp')
- grad_down: bfloat16 [16, 2048, 768], P('expert', 'dp')
Inputs may be any that keep to these rules, and one draw needn't show every extreme that they name: `route_ids`: each row names 8 different experts; every expert is named by some row. `old_owner`: each value once. `new_owner`: each value once. `capacity`: the value 24 is taken by some expert.
All inputs are finite; a program needn't handle non-finite values.
Results may differ from a plain program's by a relative error of at most 0.019.
Values may be sent and summed in bfloat16 or wider, within the bound.
A program may use at most 128 MiB of HBM per device.

v0:
```python
import math

import jax
import jax.numpy as jnp
from jax import lax
from jax.sharding import PartitionSpec as P

CAP = 24


def silu_slope(value):
    sigma = jax.nn.sigmoid(value)
    return sigma * (1.0 + value * (1.0 - sigma))


def matching(values, count):
    ranks = jnp.arange(count, dtype=jnp.int32)
    return values[:, None] == ranks[None, :]


def source_slots(old_owner, new_owner):
    settle = matching(new_owner, new_owner.shape[0])
    return jnp.sum(jnp.where(settle, old_owner[:, None], 0), axis=0)


def on_device(
    tokens,
    cotangent,
    route_ids,
    route_weights,
    capacity,
    old_owner,
    new_owner,
    w_gate,
    w_up,
    w_down,
):
    lanes = lax.axis_size("expert")
    groups = lax.axis_size("dp")
    tok_rows, top = route_ids.shape
    width = tokens.shape[1]
    ffn_width = w_gate.shape[2]
    experts = capacity.shape[0]
    slots = lanes * CAP
    contract_hidden = (((1,), (1,)), ((), ()))
    contract_rows = (((0,), (0,)), ((), ()))
    flat_ids = route_ids.reshape(-1)
    chosen = matching(flat_ids, experts).astype(jnp.int32)
    before = jnp.cumsum(chosen, axis=0) - chosen
    position = jnp.sum(before * chosen, axis=1)
    limit = jnp.sum(chosen * capacity[None, :], axis=1)
    target = jnp.sum(chosen * old_owner[None, :], axis=1)
    slot_id = jnp.where(position < limit, target * CAP + position, -1)
    match = matching(slot_id, slots).T
    match_table = match.astype(jnp.bfloat16)
    place = jnp.any(match.reshape(slots, tok_rows, top), axis=2).astype(jnp.bfloat16)
    x_send = jnp.dot(place, tokens, preferred_element_type=jnp.float32).astype(jnp.bfloat16)
    c_send = jnp.dot(place, cotangent, preferred_element_type=jnp.float32).astype(jnp.bfloat16)
    w_send = jnp.dot(
        match_table, route_weights.reshape(-1), preferred_element_type=jnp.float32
    ).astype(jnp.bfloat16)
    x_recv, c_recv, w_recv = (
        lax.all_to_all(
            x_send.reshape(lanes, CAP, width), "expert", split_axis=0, concat_axis=0, tiled=True
        ),
        lax.all_to_all(
            c_send.reshape(lanes, CAP, width), "expert", split_axis=0, concat_axis=0, tiled=True
        ),
        lax.all_to_all(
            w_send.reshape(lanes, CAP), "expert", split_axis=0, concat_axis=0, tiled=True
        ),
    )
    x_flat = x_recv.reshape(slots, width)
    c_flat = c_recv.reshape(slots, width)
    w_flat = w_recv.reshape(slots)
    gate_w = w_gate[0]
    up_w = w_up[0]
    down_w = w_down[0]
    gate = jnp.dot(x_flat, gate_w, preferred_element_type=jnp.float32)
    up = jnp.dot(x_flat, up_w, preferred_element_type=jnp.float32)
    act = jax.nn.silu(gate)
    hidden = (act * up).astype(jnp.bfloat16)
    out_rows = lax.dot_general(hidden, down_w, contract_hidden, preferred_element_type=jnp.float32)
    weight_slot = (
        jnp.sum(out_rows * c_flat.astype(jnp.float32), axis=1) / math.sqrt(width)
    ).astype(jnp.bfloat16)
    scaled = (w_flat.astype(jnp.float32)[:, None] * c_flat.astype(jnp.float32)).astype(jnp.bfloat16)
    dhidden = jnp.dot(scaled, down_w, preferred_element_type=jnp.float32)
    dgate = (dhidden * up * silu_slope(gate)).astype(jnp.bfloat16)
    dup = (dhidden * act).astype(jnp.bfloat16)
    dx_rows = lax.dot_general(dgate, gate_w, contract_hidden, preferred_element_type=jnp.float32)
    dx_rows = (
        dx_rows + lax.dot_general(dup, up_w, contract_hidden, preferred_element_type=jnp.float32)
    ).astype(jnp.bfloat16)
    dx_back, dw_back = (
        lax.all_to_all(
            dx_rows.reshape(lanes, CAP, width), "expert", split_axis=0, concat_axis=0, tiled=True
        ),
        lax.all_to_all(
            weight_slot.reshape(lanes, CAP), "expert", split_axis=0, concat_axis=0, tiled=True
        ),
    )
    grad_x = lax.dot_general(
        place, dx_back.reshape(slots, width), contract_rows, preferred_element_type=jnp.float32
    ).astype(jnp.bfloat16)
    grad_weights = (
        jnp.dot(dw_back.reshape(slots), match_table, preferred_element_type=jnp.float32)
        .reshape(tok_rows, top)
        .astype(jnp.bfloat16)
    )
    grad_scale = 1.0 / math.sqrt(groups * lanes * CAP)

    def product_term(left, right):
        return (
            lax.dot_general(left, right, contract_rows, preferred_element_type=jnp.float32)
            * grad_scale
        )

    summed = lax.psum_scatter(
        jnp.concatenate(
            [product_term(x_flat, dgate), product_term(x_flat, dup), product_term(scaled, hidden)],
            axis=1,
        ).astype(jnp.bfloat16),
        "dp",
        scatter_dimension=0,
        tiled=True,
    )
    placed_from = source_slots(old_owner, new_owner)
    wanted = jnp.sum(
        jnp.where(jnp.arange(lanes, dtype=jnp.int32) == lax.axis_index("expert"), placed_from, 0)
    )
    piece = lax.all_gather(summed[None], "expert", axis=0, tiled=True)
    index_now = jnp.arange(piece.shape[0], dtype=jnp.int32)
    picked = jnp.where((index_now == wanted)[:, None, None], piece.astype(jnp.float32), 0.0)
    moved = jnp.sum(picked, axis=0).astype(jnp.bfloat16)
    grad_gate = moved[:, :ffn_width][None]
    grad_up = moved[:, ffn_width : 2 * ffn_width][None]
    grad_down = moved[:, 2 * ffn_width :][None]
    return (grad_x, grad_weights, grad_gate, grad_up, grad_down)


def solution(mesh):
    return jax.shard_map(
        on_device,
        mesh=mesh,
        in_specs=(
            P(("dp", "expert"), None),
            P(("dp", "expert"), None),
            P(("dp", "expert"), None),
            P(("dp", "expert"), None),
            P(),
            P(),
            P(),
            P("expert", None, None),
            P("expert", None, None),
            P("expert", None, None),
        ),
        out_specs=(
            P(("dp", "expert"), None),
            P(("dp", "expert"), None),
            P("expert", "dp", None),
            P("expert", "dp", None),
            P("expert", "dp", None),
        ),
        check_vma=False,
    )
```

profile of v0, /device:TPU:1, one launch (start us, length us, event | category | flops | bytes accessed | tf_op | source)
XLA Modules:
  0.0 380.6 jit_solution(7078463080024469864)
XLA Ops:
  8.4 4.5 %reduce-window.6 = s32[16,16,128]{2,1,0:T(8,128)S(1)} reduce-window(s32[16,16,128]{2,1,0:T(8,128)S(1)} %fusion.32, s32[]{:T(128)} %constant.9.clone.1), window={size=1x1x128 pad=0_0x0_0x127_0}, to_apply=%region_0.0 | reduce-window | flops 4161536 | bytes 262148 | tf_op jit(solution)/shard_map/reduce-window
  16.7 7.3 %all-to-all-start = ((bf16[16,1,24]{2,1,0:T(2,128)(2,1)}), bf16[16,1,24]{2,1,0:T(2,128)(2,1)S(1)}, u32[]{:S(2)}, u32[]{:S(2)}) async-start(bf16[16,1,24]{2,1,0:T(2,128)(2,1)} %all_to_all.25), calls=%async_computation | async-start | bytes 16384 | tf_op jit(solution)/shard_map/all_to_all | solution.py:69
  25.6 3.0 convolution_convert_fusion
  29.5 4.8 %all-to-all-start.2 = ((bf16[16,24,2048]{2,1,0:T(8,128)(2,1)}), bf16[16,24,2048]{2,1,0:T(8,128)(2,1)}, u32[]{:S(2)}, u32[]{:S(2)}) async-start(bf16[16,24,2048]{2,1,0:T(8,128)(2,1)} %bitcast.95), calls=%async_computation.2 | async-start | bytes 3145728 | tf_op jit(solution)/shard_map/all_to_all | solution.py:63
  34.3 3.0 convolution_convert_fusion.1
  37.2 18.7 %all-to-all-done.2 = bf16[16,24,2048]{2,1,0:T(8,128)(2,1)} async-done(((bf16[16,24,2048]{2,1,0:T(8,128)(2,1)}), bf16[16,24,2048]{2,1,0:T(8,128)(2,1)}, u32[]{:S(2)}, u32[]{:S(2)}) %all-to-all-start.2) | async-done | bytes 1572896 | tf_op jit(solution)/shard_map/all_to_all | solution.py:63
  56.0 5.0 %all-to-all-start.1 = ((bf16[16,24,2048]{2,1,0:T(8,128)(2,1)}), bf16[16,24,2048]{2,1,0:T(8,128)(2,1)}, u32[]{:S(2)}, u32[]{:S(2)}) async-start(bf16[16,24,2048]{2,1,0:T(8,128)(2,1)} %bitcast.94), calls=%async_computation.1 | async-start | bytes 3145728 | tf_op jit(solution)/shard_map/all_to_all | solution.py:66
  61.3 4.8 %fusion.6 = f32[384,768]{1,0:T(8,128)} fusion(bf16[384,2048]{1,0:T(8,128)(2,1)} %bitcast.6, bf16[1,2048,768]{2,1,0:T(8,128)(2,1)} %param.17), kind=kOutput, calls=%fused_computation.15 | convolution fusion | flops 1207959552 | bytes 5898240 | tf_op jit(solution)/shard_map/dot_general | solution.py:79
  66.1 16.6 %all-to-all-done.1 = bf16[16,24,2048]{2,1,0:T(8,128)(2,1)} async-done(((bf16[16,24,2048]{2,1,0:T(8,128)(2,1)}), bf16[16,24,2048]{2,1,0:T(8,128)(2,1)}, u32[]{:S(2)}, u32[]{:S(2)}) %all-to-all-start.1) | async-done | bytes 1572896 | tf_op jit(solution)/shard_map/all_to_all | solution.py:66
  82.7 1.9 fusion.1
  86.5 3.1 multiply_convert_fusion.3
  89.6 3.9 %multiply_convert_fusion.1 = bf16[2048,768]{0,1:T(8,128)(2,1)S(1)} fusion(bf16[384,2048]{1,0:T(8,128)(2,1)} %bitcast.6, bf16[384,768]{1,0:T(8,128)(2,1)S(1)} %get-tuple-element.25), kind=kOutput, calls=%fused_computation.5 | convolution fusion | flops 1211105280 | bytes 5308416 | tf_op jit(solution)/shard_map/dot_general | solution.py:115
  93.5 3.3 multiply_convert_fusion.2
  96.8 1.7 fusion.3
  98.5 1.9 multiply_convert_fusion
  100.4 4.4 %pad_maximum_fusion = bf16[2048,2304]{0,1:T(8,128)(2,1)} fusion(bf16[2048,768]{0,1:T(8,128)(2,1)S(1)} %multiply_convert_fusion, bf16[2048,768]{0,1:T(8,128)(2,1)S(1)} %multiply_convert_fusion.1, bf16[2048,768]{0,1:T(8,128)(2,1)S(1)} %multiply_convert_fusion.2), kind=kLoop, calls=%fused_computation.3 | loop fusion | flops 28311552 | bytes 18874368 | tf_op jit(solution)/shard_map/concatenate | solution.py:120
  104.8 12.2 %copy.43 = bf16[2048,2304]{1,0:T(8,128)(2,1)} copy(bf16[2048,2304]{0,1:T(8,128)(2,1)} %pad_maximum_fusion) | data formatting | bytes 18874368
  117.1 130.5 %reduce-scatter.4.cloned.1.call-done = bf16[128,2304]{1,0:T(8,128)(2,1)} async-done(((bf16[2048,2304]{1,0:T(8,128)(2,1)}), bf16[128,2304]{1,0:T(8,128)(2,1)}) %reduce-scatter.4.cloned.1.call-update) | async-done | bytes 589840
  247.6 2.1 copy.44
  249.7 4.0 %fusion.2 = f32[384]{0:T(512)S(1)} fusion(bf16[16,24,2048]{2,1,0:T(8,128)(2,1)} %all-to-all-done.1, bf16[384,768]{1,0:T(8,128)(2,1)} %copy-done.8, bf16[1,2048,768]{2,1,0:T(8,128)(2,1)} %param.19), kind=kOutput, calls=%fused_computation.11 | convolution fusion | flops 1210318464 | bytes 5309952 | tf_op jit(solution)/shard_map/dot_general | solution.py:83
  254.4 5.7 %all-to-all-start.4 = ((bf16[16,1,24]{2,1,0:T(2,128)(2,1)}), bf16[16,1,24]{2,1,0:T(2,128)(2,1)S(1)}, u32[]{:S(2)}, u32[]{:S(2)}) async-start(bf16[16,1,24]{2,1,0:T(2,128)(2,1)} %convert_element_type.120), calls=%async_computation.4 | async-start | bytes 16384 | tf_op jit(solution)/shard_map/all_to_all | solution.py:99
  260.2 3.6 fusion.4
  263.8 2.6 add_convert_fusion
  266.4 5.9 %all-to-all-start.3 = ((bf16[16,24,2048]{2,1,0:T(8,128)(2,1)}), bf16[16,24,2048]{2,1,0:T(8,128)(2,1)}, u32[]{:S(2)}, u32[]{:S(2)}) async-start(bf16[16,24,2048]{2,1,0:T(8,128)(2,1)} %bitcast.96), calls=%async_computation.3 | async-start | bytes 3145728 | tf_op jit(solution)/shard_map/all_to_all | solution.py:96
  273.8 4.8 %fusion.19 = bf16[1,256,8]{2,0,1:T(2,128)(2,1)S(1)} fusion(bf16[384,1,1]{0,1,2:T(2,128)(2,1)S(1)} %reshape.166, s32[256,8]{1,0:T(8,128)S(1)} %select_n.26), kind=kOutput, calls=%fused_computation.32 | convolution fusion | flops 2359296 | bytes 13056 | tf_op jit(solution)/shard_map/dot_general | solution.py:107
  279.3 23.4 %all-to-all-done.3 = bf16[16,24,2048]{2,1,0:T(8,128)(2,1)} async-done(((bf16[16,24,2048]{2,1,0:T(8,128)(2,1)}), bf16[16,24,2048]{2,1,0:T(8,128)(2,1)}, u32[]{:S(2)}, u32[]{:S(2)}) %all-to-all-start.3) | async-done | bytes 1572896 | tf_op jit(solution)/shard_map/all_to_all | solution.py:96
  302.6 3.2 convolution_convert_fusion.2
  305.8 28.4 %all-gather.3.cloned.1.call-done = bf16[2048,2304]{0,1:T(8,128)(2,1)} async-done(((bf16[128,2304]{0,1:T(8,128)(2,1)}), bf16[2048,2304]{0,1:T(8,128)(2,1)}) %all-gather.3.cloned.1.call-update) | async-done | bytes 9437200 | tf_op jit(solution)/shard_map/all_gather | solution.py:132
  334.2 12.6 %convert_bitcast_fusion = f32[288,8,16,128]{3,1,2,0:T(8,128)} fusion(bf16[2048,2304]{0,1:T(8,128)(2,1)} %all-gather.3.cloned.1.call-done), kind=kLoop, calls=%fused_computation.2 | loop fusion | flops 4718592 | bytes 28311552
  346.9 10.3 %copy.46 = f32[288,8,16,128]{3,2,1,0:T(8,128)S(1)} copy(f32[288,8,16,128]{3,1,2,0:T(8,128)} %convert_bitcast_fusion) | data formatting | bytes 37748736
  357.1 12.5 %fusion = bf16[128,2304]{0,1:T(8,128)(2,1)S(1)} fusion(f32[288,8,16,128]{3,2,1,0:T(8,128)S(1)} %copy.46, pred[16]{0:T(512)(128)(4,1)S(1)} %iota_compare_fusion.9), kind=kLoop, calls=%fused_computation.1 | loop fusion | flops 9142272 | bytes 19464208 | tf_op jit(solution)/shard_map/reduce_sum | solution.py:135
  370.4 1.7 copy.39
  (55 shorter events, 15.0 us)
Async XLA Ops:
  7.2 79.3 %copy-start = (bf16[1,2048,768]{2,1,0:T(8,128)(2,1)S(1)}, bf16[1,2048,768]{2,1,0:T(8,128)(2,1)}, u32[]{:S(2)}) copy-start(bf16[1,2048,768]{2,1,0:T(8,128)(2,1)} %param.18) | copy-start | bytes 9437188
  16.7 12.7 %all-to-all-start = ((bf16[16,1,24]{2,1,0:T(2,128)(2,1)}), bf16[16,1,24]{2,1,0:T(2,128)(2,1)S(1)}, u32[]{:S(2)}, u32[]{:S(2)}) async-start(bf16[16,1,24]{2,1,0:T(2,128)(2,1)} %all_to_all.25), calls=%async_computation | async-start | bytes 16384 | tf_op jit(solution)/shard_map/all_to_all | solution.py:69
  29.5 26.5 %all-to-all-start.2 = ((bf16[16,24,2048]{2,1,0:T(8,128)(2,1)}), bf16[16,24,2048]{2,1,0:T(8,128)(2,1)}, u32[]{:S(2)}, u32[]{:S(2)}) async-start(bf16[16,24,2048]{2,1,0:T(8,128)(2,1)} %bitcast.95), calls=%async_computation.2 | async-start | bytes 3145728 | tf_op jit(solution)/shard_map/all_to_all | solution.py:63
  56.0 26.7 %all-to-all-start.1 = ((bf16[16,24,2048]{2,1,0:T(8,128)(2,1)}), bf16[16,24,2048]{2,1,0:T(8,128)(2,1)}, u32[]{:S(2)}, u32[]{:S(2)}) async-start(bf16[16,24,2048]{2,1,0:T(8,128)(2,1)} %bitcast.94), calls=%async_computation.1 | async-start | bytes 3145728 | tf_op jit(solution)/shard_map/all_to_all | solution.py:66
  61.0 186.6 %reduce-scatter.4.cloned.1.call-start = ((), (), s32[]{:S(2)}) async-start(), calls=%async_computation.7 | async-start | bytes 10027008
  82.7 2.4 copy-start.2
  85.0 1.4 copy-start.6
  89.6 3.9 %copy-start.4 = (bf16[384,768]{1,0:T(8,128)(2,1)}, bf16[384,768]{1,0:T(8,128)(2,1)S(1)}, u32[]{:S(2)}) copy-start(bf16[384,768]{1,0:T(8,128)(2,1)S(1)} %get-tuple-element.25) | copy-start | bytes 1769476
  89.6 3.9 %copy-start.7 = (bf16[384,768]{1,0:T(8,128)(2,1)}, bf16[384,768]{1,0:T(8,128)(2,1)S(1)}, u32[]{:S(2)}) copy-start(bf16[384,768]{1,0:T(8,128)(2,1)S(1)} %get-tuple-element.24) | copy-start | bytes 1769476
  89.6 8.9 %copy-start.8 = (bf16[384,768]{1,0:T(8,128)(2,1)}, bf16[384,768]{1,0:T(8,128)(2,1)S(1)}, u32[]{:S(2)}) copy-start(bf16[384,768]{1,0:T(8,128)(2,1)S(1)} %get-tuple-element.23) | copy-start | bytes 1769476
  117.0 217.2 %all-gather.3.cloned.1.call-start = ((), (), s32[]{:S(2)}) async-start(), calls=%async_computation.6 | async-start | bytes 10027008 | tf_op jit(solution)/shard_map/all_gather | solution.py:132
  254.4 12.0 %all-to-all-start.4 = ((bf16[16,1,24]{2,1,0:T(2,128)(2,1)}), bf16[16,1,24]{2,1,0:T(2,128)(2,1)S(1)}, u32[]{:S(2)}, u32[]{:S(2)}) async-start(bf16[16,1,24]{2,1,0:T(2,128)(2,1)} %convert_element_type.120), calls=%async_computation.4 | async-start | bytes 16384 | tf_op jit(solution)/shard_map/all_to_all | solution.py:99
  260.2 3.6 copy-start.5
  266.4 5.9 %copy-start.1 = (s32[16]{0:T(128)S(1)}, s32[16]{0:T(128)}, u32[]{:S(2)}) copy-start(s32[16]{0:T(128)} %param.15) | copy-start | bytes 196
  266.4 5.9 %copy-start.3 = (s32[16]{0:T(128)S(1)}, s32[16]{0:T(128)}, u32[]{:S(2)}) copy-start(s32[16]{0:T(128)} %param.16) | copy-start | bytes 196
  266.4 36.2 %all-to-all-start.3 = ((bf16[16,24,2048]{2,1,0:T(8,128)(2,1)}), bf16[16,24,2048]{2,1,0:T(8,128)(2,1)}, u32[]{:S(2)}, u32[]{:S(2)}) async-start(bf16[16,24,2048]{2,1,0:T(8,128)(2,1)} %bitcast.96), calls=%async_computation.3 | async-start | bytes 3145728 | tf_op jit(solution)/shard_map/all_to_all | solution.py:96
Sparse Core Ops, SparseCore 0:
  117.1 130.3 reduce-scatter.3
  249.8 84.3 all-gather.2
where the time goes:
time: 382 us; the launch traced here: 381 us
  waiting for transfers between devices  218 us (57%)
  matrix products  42.9 us (11%)
  other arithmetic  41.7 us (11%)
  local copies, waits for them, and re-layouts  34.2 us (9%)
  starting transfers between devices  29 us (8%)
  between operations  14.3 us (4%)
    unnamed x3, waiting for transfers between devices  131 us
    unnamed x26, local copies, waits for them, and re-layouts  30.2 us
    all_gather x1, waiting for transfers between devices, on_device(): piece = lax.all_gather(summed[None], 'expert', axis=0, tiled=True)  28.4 us
    all_to_all x1, waiting for transfers between devices, on_device(): lax.all_to_all(dx_rows.reshape(lanes, CAP, width), 'expert', split_axis=0...  23.4 us
    all_to_all x1, waiting for transfers between devices, on_device(): lax.all_to_all(x_send.reshape(lanes, CAP, width), 'expert', split_axis=0,...  18.7 us
    all_to_all x1, waiting for transfers between devices, on_device(): lax.all_to_all(c_send.reshape(lanes, CAP, width), 'expert', split_axis=0,...  16.6 us
    unnamed x1, other arithmetic  12.6 us
    reduce_sum x1, other arithmetic, on_device(): moved = jnp.sum(picked, axis=0).astype(jnp.bfloat16)  12.5 us
  transfers between devices with their start and end apart: 7, of which 6 were waited for; matrix products, arithmetic and copies ran while one was open for 9% of the time, Pallas kernels for 0%

commit v1 on v0

v1 whole, which is shorter than its diff:
```python
import math

import jax
import jax.numpy as jnp
from jax import lax
from jax.experimental import pallas as pl
from jax.experimental.pallas import tpu as pltpu
from jax.sharding import PartitionSpec as P

MESH = pl.DeviceIdType.MESH
CAP = 24
LANES = 16
TOK = 256
D = 2048
FFN = 768
ROWS = LANES * CAP
PAIR = 2 * CAP
COLS = 256
CHUNKS = FFN // COLS
UNITS = 6 * CHUNKS
XBLK = D // 4
ZBLK = XBLK // 4
BF = jnp.bfloat16
F32 = jnp.float32
NT = (((1,), (1,)), ((), ()))


def iota(shape, dim):
    return lax.broadcasted_iota(jnp.int32, shape, dim)


def eye(n):
    return (iota((n, n), 0) == iota((n, n), 1)).astype(F32).astype(BF)


def dot(a, b):
    return jnp.dot(a, b, preferred_element_type=F32)


def dot_nt(a, b):
    return lax.dot_general(a, b, NT, preferred_element_type=F32)


def body(
    tok, cot, ids, rw, cap, old, old_s, new_s, wg_h, wu_h, wd_h,
    gx, gw, gg, gu, gd,
    wg, wu, wd, xs_send, xs_recv, xb, sb, hb, pb, xr, zb, zr,
    dx_send, dx_recv, ws_send, ws_recv, place_l, place_r, gbuf, p1a, p1b, p1c, p2, ob, wanted,
    w_sem, d_ss, d_rs, x_ss, x_rs, z_ss, z_rs, b_ss, b_rs, v_ss, v_rs, p_ss, p_rs, q_ss, q_rs,
):
    dp = lax.axis_index("dp")
    me = lax.axis_index("expert")
    x, zh = dp // 4, dp % 4
    y, zl, co = me // 4, (me // 2) % 2, me % 2
    p1 = (p1a, p1b, p1c)

    def at_x(s):
        return (((x + s + 4) % 4) * 4 + zh, me)

    def at_z(s):
        return (x * 4 + (zh + s + 4) % 4, me)

    def ahead(k):
        return ((y + k // 4) % 4) * 4 + ((zl + (k // 2) % 2) % 2) * 2 + (co + k % 2) % 2

    def behind(k):
        return ((y + 4 - k // 4) % 4) * 4 + ((zl + (k // 2) % 2) % 2) * 2 + (co + k % 2) % 2

    def remote(src, dst, ss, rs, device):
        return pltpu.make_async_remote_copy(
            src_ref=src, dst_ref=dst, send_sem=ss, recv_sem=rs,
            device_id=device, device_id_type=MESH,
        )

    def each_peer(step):
        def run(i, carry):
            step(LANES - i)
            return carry

        lax.fori_loop(1, LANES, run, 0)

    weights = [
        pltpu.make_async_copy(h.at[0], v, w_sem.at[i])
        for i, (h, v) in enumerate(((wg_h, wg), (wu_h, wu), (wd_h, wd)))
    ]
    for copy in weights:
        copy.start()
    barrier = pltpu.get_barrier_semaphore()

    def greet(k):
        pl.semaphore_signal(barrier, inc=1, device_id=(dp, ahead(k)), device_id_type=MESH)

    each_peer(greet)
    for s in (1, -1):
        pl.semaphore_signal(barrier, inc=1, device_id=at_x(s), device_id_type=MESH)
        pl.semaphore_signal(barrier, inc=1, device_id=at_z(s), device_id_type=MESH)

    ids_t = dot_nt(eye(8), ids[...].astype(F32).astype(BF))
    rw_t = dot_nt(eye(8), rw[...])
    mine = old[...] == iota((LANES, LANES), 0)
    ex = jnp.sum(jnp.where(mine, iota((LANES, LANES), 1), 0).astype(F32), axis=1, keepdims=True)
    limit = jnp.sum(jnp.where(mine, cap[...], 0).astype(F32), axis=1, keepdims=True)
    named = jnp.zeros((LANES, TOK), F32)
    w_sel = jnp.zeros((LANES, TOK), F32)
    for k in range(8):
        hit = ids_t[k : k + 1, :] == ex
        named = named + jnp.where(hit, 1.0, 0.0)
        w_sel = w_sel + jnp.where(hit, rw_t[k : k + 1, :], 0.0)
    earlier = (iota((TOK, TOK), 0) < iota((TOK, TOK), 1)).astype(F32).astype(BF)
    before = dot(named.astype(BF), earlier)
    pos = jnp.where((named > 0.5) & (before < limit), before, -1.0)
    p_of = iota((CAP, TOK), 0).astype(F32)
    nothing = jnp.zeros((CAP, TOK), F32)
    ones, weighted, left, right = [], [], [], []
    for s in range(LANES):
        one = jnp.where(pos[s : s + 1, :] == p_of, 1.0, 0.0)
        ones.append(one)
        weighted.append(one * w_sel[s : s + 1, :])
        left += [one, nothing]
        right += [nothing, one]
    place = jnp.concatenate(ones, axis=0).astype(BF)
    place_w = jnp.concatenate(weighted, axis=0).astype(BF)
    place_l[...] = jnp.concatenate(left, axis=0).astype(BF)
    place_r[...] = jnp.concatenate(right, axis=0).astype(BF)
    for c in range(D // 256):
        cols = slice(256 * c, 256 * c + 256)
        rows_x = dot(place, tok[:, cols])
        rows_s = dot(place_w, cot[:, cols])
        both = []
        for s in range(LANES):
            both += [rows_x[CAP * s : CAP * s + CAP], rows_s[CAP * s : CAP * s + CAP]]
        xs_send[:, cols] = jnp.concatenate(both, axis=0).astype(BF)

    pl.semaphore_wait(barrier, LANES - 1 + 4)

    def dispatch(k):
        to = ahead(k)
        return remote(
            xs_send.at[pl.ds(pl.multiple_of(PAIR * to, 16), PAIR)],
            xs_recv.at[pl.ds(pl.multiple_of(PAIR * k, 16), PAIR)],
            d_ss.at[k], d_rs.at[k], (dp, to),
        )

    each_peer(lambda k: dispatch(k).start())
    xs_recv[0:PAIR] = xs_send[pl.ds(pl.multiple_of(PAIR * me, 16), PAIR)]

    def look_up(j, carry):
        slot = jnp.int32(0)
        for n in range(LANES):
            slot = slot + jnp.where(new_s[n] == j, old_s[n], 0)
        wanted[j] = slot
        return carry

    lax.fori_loop(0, LANES, look_up, 0)
    for copy in weights:
        copy.wait()
    each_peer(lambda k: dispatch(k).wait_recv())

    for c in range(D // 256):
        cols = slice(256 * c, 256 * c + 256)
        both = xs_recv[:, cols].astype(F32)
        xb[:, cols] = jnp.concatenate(
            [both[PAIR * k : PAIR * k + CAP] for k in range(LANES)], axis=0
        ).astype(BF)
        sb[:, cols] = jnp.concatenate(
            [both[PAIR * k + CAP : PAIR * k + PAIR] for k in range(LANES)], axis=0
        ).astype(BF)

    def hidden_chunk(c, ws):
        cols = slice(COLS * c, COLS * c + COLS)
        gate = dot(xb[...], wg[:, cols])
        up = dot(xb[...], wu[:, cols])
        dh = dot(sb[...], wd[:, cols])
        sig = 1.0 / (1.0 + jnp.exp(-gate))
        act = gate * sig
        hidden = (act * up).astype(BF)
        hb[2, :, cols] = hidden
        hb[0, :, cols] = (dh * up * (sig * (1.0 + gate * (1.0 - sig)))).astype(BF)
        hb[1, :, cols] = (dh * act).astype(BF)
        return ws + jnp.sum(hidden.astype(F32) * dh, axis=1, keepdims=True)

    scale = 1.0 / math.sqrt(4 * 4 * LANES * CAP)

    def sign(u):
        return 1 if u % 2 == 0 else -1

    def x_block(u, k):
        return (x - sign(u) * (1 + k) + 8) % 4

    def z_block(u, k):
        return (zh - sign(u) * (1 + k) + 8) % 4

    def x_copy(u, k):
        return remote(
            pb.at[u, x_block(u, k)], xr.at[k, u], x_ss.at[k, u], x_rs.at[k, u], at_x(sign(u))
        )

    def z_copy(u, k):
        return remote(
            zb.at[u, z_block(u, k)], zr.at[k, u], z_ss.at[k, u], z_rs.at[k, u], at_z(sign(u))
        )

    def units_of(j):
        return (2 * j, 2 * j + 1)

    def product(j):
        c, m = j // 3, j % 3
        turned = hb[m, :, COLS * c : COLS * c + COLS].astype(F32).T.astype(BF)
        rows = sb if m == 2 else xb
        for q in range(4):
            part = (dot(turned, rows[:, XBLK * q : XBLK * q + XBLK]) * scale).astype(BF)
            for h, u in enumerate(units_of(j)):
                pb[u, q] = part[128 * h : 128 * h + 128]
        for u in units_of(j):
            x_copy(u, 0).start()

    def x_step(j, k):
        for u in units_of(j):
            x_copy(u, k - 1).wait_recv()
            b = x_block(u, k)
            pb[u, b] = (pb[u, b].astype(F32) + xr[k - 1, u].astype(F32)).astype(BF)
            x_copy(u, k).start()
            x_copy(u, k - 1).wait_send()

    def x_last(j):
        for u in units_of(j):
            x_copy(u, 2).wait_recv()
            total = (pb[u, x].astype(F32) + xr[2, u].astype(F32)).astype(BF)
            for q in range(4):
                zb[u, q] = total[:, ZBLK * q : ZBLK * q + ZBLK]
            z_copy(u, 0).start()
            x_copy(u, 2).wait_send()

    def z_step(j, k):
        for u in units_of(j):
            z_copy(u, k - 1).wait_recv()
            b = z_block(u, k)
            zb[u, b] = (zb[u, b].astype(F32) + zr[k - 1, u].astype(F32)).astype(BF)
            z_copy(u, k).start()
            z_copy(u, k - 1).wait_send()

    def z_last(j):
        for u in units_of(j):
            z_copy(u, 2).wait_recv()
            total = zb[u, zh].astype(F32) + zr[2, u].astype(F32)
            gbuf[u // 6, u % 6] = total.T.astype(BF)
            z_copy(u, 2).wait_send()

    def piece(n):
        return pl.ds(3 * (n % 2), 3), pl.ds(pl.multiple_of(16 * (n // 2), 16), 16)

    def out_copy(g, k):
        to = ahead(k)
        us, rs = piece(to)
        return remote(
            gbuf.at[g, us, rs], p1[g].at[me], p_ss.at[g, k], p_rs.at[g, k], (dp, to)
        )

    def in_copy(g, k):
        to = ahead(k)
        us, rs = piece(me)
        return remote(p2.at[g, to], ob.at[g, us, rs], q_ss.at[g, k], q_rs.at[g, k], (dp, to))

    def move_out(g):
        each_peer(lambda k: out_copy(g, k).start())
        us, rs = piece(me)
        p1[g][me] = gbuf[g, us, rs]

    def move_pick(g):
        each_peer(lambda k: out_copy(g, k).wait_recv())

        def pick(j, carry):
            p2[g, j] = p1[g][wanted[j]]
            return carry

        lax.fori_loop(0, LANES, pick, 0)
        each_peer(lambda k: in_copy(g, k).start())
        us, rs = piece(me)
        ob[g, us, rs] = p2[g, me]
        each_peer(lambda k: out_copy(g, k).wait_send())

    def move_in(g):
        each_peer(lambda k: in_copy(g, k).wait_recv())
        for m, out in enumerate((gg, gu, gd)):
            for h in range(2):
                at = COLS * g + 128 * h
                out[0, :, at : at + 128] = ob[g, 2 * m + h]
        each_peer(lambda k: in_copy(g, k).wait_send())

    def back_copy(k):
        to = behind(k)
        return remote(
            dx_send.at[pl.ds(pl.multiple_of(PAIR * k, 16), PAIR)],
            dx_recv.at[pl.ds(pl.multiple_of(PAIR * me, 16), PAIR)],
            b_ss.at[k], b_rs.at[k], (dp, to),
        )

    def value_copy(k):
        return remote(ws_send.at[k], ws_recv.at[me], v_ss.at[k], v_rs.at[k], (dp, behind(k)))

    diagonal = iota((CAP, 128), 0) == iota((CAP, 128), 1)

    def send_back(ws):
        ws = ws / math.sqrt(D)
        for k in range(LANES):
            row = jnp.sum(
                jnp.where(diagonal, ws[CAP * k : CAP * k + CAP], 0.0), axis=0, keepdims=True
            )
            ws_send[k] = jnp.broadcast_to(row, (8, 128))
        for c in range(4):
            halves = []
            for half in range(2):
                at = 1024 * half + 256 * c
                halves.append(
                    dot_nt(hb[0], wg[at : at + 256, :]) + dot_nt(hb[1], wu[at : at + 256, :])
                )
            both = []
            for k in range(LANES):
                both += [part[CAP * k : CAP * k + CAP] for part in halves]
            dx_send[:, 256 * c : 256 * c + 256] = jnp.concatenate(both, axis=0).astype(BF)

        def start(k):
            back_copy(k).start()
            value_copy(k).start()

        each_peer(start)
        dx_recv[pl.ds(pl.multiple_of(PAIR * me, 16), PAIR)] = dx_send[0:PAIR]
        ws_recv[me] = ws_send[0]

    def combine():
        def arrived(k):
            back_copy(k).wait_recv()
            value_copy(k).wait_recv()

        each_peer(arrived)
        for half, table in enumerate((place_l, place_r)):
            turned = table[...].astype(F32).T.astype(BF)
            for c in range(2):
                at = 1024 * half + 512 * c
                gx[:, at : at + 512] = dot(turned, dx_recv[:, 512 * c : 512 * c + 512]).astype(BF)
        chosen = []
        for s in range(LANES):
            column = jnp.sum(
                jnp.where(diagonal, ws_recv[s, 0:1, :], 0.0), axis=1, keepdims=True
            )
            one = place_l[PAIR * s : PAIR * s + PAIR].astype(F32)[0:CAP]
            chosen.append(jnp.sum(one * column, axis=0, keepdims=True))
        chosen = jnp.concatenate(chosen, axis=0)
        parts = [
            jnp.sum(jnp.where(ids_t[k : k + 1, :] == ex, chosen, 0.0), axis=0, keepdims=True)
            for k in range(8)
        ]
        values = (jnp.concatenate(parts, axis=0) / rw_t).astype(BF)
        gw[...] = dot_nt(eye(TOK), values).astype(BF)

        def left(k):
            back_copy(k).wait_send()
            value_copy(k).wait_send()

        each_peer(left)

    ws = hidden_chunk(0, jnp.zeros((ROWS, 1), F32))
    for j in range(3):
        product(j)
    ws = hidden_chunk(1, ws)
    ws = hidden_chunk(2, ws)
    send_back(ws)
    for g in range(3):
        now = range(3 * g, 3 * g + 3)
        last = range(3 * g - 3, 3 * g) if g else ()
        for j in now:
            x_step(j, 1)
        for j in last:
            z_step(j, 1)
        for j in now:
            x_step(j, 2)
        if g < 2:
            for j in now:
                product(j + 3)
        for j in last:
            z_step(j, 2)
        if g == 0:
            combine()
        for j in now:
            x_last(j)
        for j in last:
            z_last(j)
        if g:
            move_out(g - 1)
        if g > 1:
            move_in(g - 2)
        if g:
            move_pick(g - 1)
    for j in range(6, 9):
        z_step(j, 1)
    for j in range(6, 9):
        z_step(j, 2)
    for j in range(6, 9):
        z_last(j)
    move_out(2)
    move_in(1)
    each_peer(lambda k: dispatch(k).wait_send())
    move_pick(2)
    move_in(2)


def on_device(
    tokens, cotangent, route_ids, route_weights, capacity, old_owner, new_owner, w_gate, w_up, w_down
):
    vmem = pl.BlockSpec(memory_space=pltpu.VMEM)
    smem = pl.BlockSpec(memory_space=pltpu.SMEM)
    hbm = pl.BlockSpec(memory_space=pl.ANY)
    dma = pltpu.SemaphoreType.DMA
    shard = jax.ShapeDtypeStruct((1, 128, FFN), BF)
    V = pltpu.VMEM
    return pl.pallas_call(
        body,
        out_shape=(
            jax.ShapeDtypeStruct((TOK, D), BF),
            jax.ShapeDtypeStruct((TOK, 8), BF),
            shard, shard, shard,
        ),
        in_specs=[vmem] * 6 + [smem] * 2 + [hbm] * 3,
        out_specs=[vmem] * 5,
        scratch_shapes=[
            V((D, FFN), BF), V((D, FFN), BF), V((D, FFN), BF),
            V((2 * ROWS, D), BF), V((2 * ROWS, D), BF),
            V((ROWS, D), BF), V((ROWS, D), BF), V((3, ROWS, FFN), BF),
            V((UNITS, 4, 128, XBLK), BF), V((3, UNITS, 128, XBLK), BF),
            V((UNITS, 4, 128, ZBLK), BF), V((3, UNITS, 128, ZBLK), BF),
            V((2 * ROWS, D // 2), BF), V((2 * ROWS, D // 2), BF),
            V((LANES, 8, 128), F32), V((LANES, 8, 128), F32),
            V((2 * ROWS, TOK), BF), V((2 * ROWS, TOK), BF),
            V((3, 6, 128, 128), BF),
            V((LANES, 3, 16, 128), BF), V((LANES, 3, 16, 128), BF), V((LANES, 3, 16, 128), BF),
            V((3, LANES, 3, 16, 128), BF),
            V((3, 6, 128, 128), BF),
            pltpu.SMEM((LANES,), jnp.int32),
            dma((3,)),
            dma((LANES,)), dma((LANES,)),
            dma((3, UNITS)), dma((3, UNITS)),
            dma((3, UNITS)), dma((3, UNITS)),
            dma((LANES,)), dma((LANES,)), dma((LANES,)), dma((LANES,)),
            dma((3, LANES)), dma((3, LANES)), dma((3, LANES)), dma((3, LANES)),
        ],
        compiler_params=pltpu.CompilerParams(
            collective_id=0, has_side_effects=True, vmem_limit_bytes=62 * 1024 * 1024
        ),
        name="moe",
    )(
        tokens, cotangent, route_ids, route_weights,
        capacity[None], old_owner[None], old_owner, new_owner,
        w_gate, w_up, w_down,
    )


def solution(mesh):
    rows = P(("dp", "expert"), None)
    slots = P("expert", None, None)
    shards = P("expert", "dp", None)
    return jax.shard_map(
        on_device,
        mesh=mesh,
        in_specs=(rows, rows, rows, rows, P(), P(), P(), slots, slots, slots),
        out_specs=(rows, rows, shards, shards, shards),
        check_vma=False,
    )
```

time: 382 us -> 177 us (0.46)
  waiting for transfers between devices: 218 us -> 0 us
  Pallas kernels: 0 us -> 165 us
  matrix products: 42.9 us -> 0 us
  other arithmetic: 41.7 us -> 0 us
  starting transfers between devices: 29 us -> 0 us
  local copies, waits for them, and re-layouts: 34.2 us -> 11.6 us
  between operations: 14.3 us -> 0.64 us
    pallas_call x0 -> x1, Pallas kernels: none -> 165 us  [on_device(): pl.pallas_call(body, out_shape=(jax.ShapeDtypeStruct((TOK, D), BF), jax.S...]
    unnamed x3 -> x0, waiting for transfers between devices: 131 us -> none
    all_to_all x5 -> x0, waiting for transfers between devices: 59.5 us -> none  [the longest x1 23.4 us: on_device(): lax.all_to_all(dx_rows.reshape(lanes, CAP, width), 'expert', split_axis=0...]
    dot_general x14 -> x0, matrix products: 42.9 us -> none  [the longest x3 9.01 us: product_term(): lax.dot_general(left, right, contract_rows, preferred_element_type=jnp.fl...]
    all_to_all x5 -> x0, starting transfers between devices: 28.8 us -> none  [the longest x1 7.34 us: on_device(): lax.all_to_all(w_send.reshape(lanes, CAP), 'expert', split_axis=0, concat...]
    all_gather x1 -> x0, waiting for transfers between devices: 28.4 us -> none  [on_device(): piece = lax.all_gather(summed[None], 'expert', axis=0, tiled=True)]
    unnamed x26 -> x6, local copies, waits for them, and re-layouts: 30.2 us -> 10.1 us
    reduce_sum x4 -> x0, other arithmetic: 14 us -> none  [the longest x1 12.5 us: on_device(): moved = jnp.sum(picked, axis=0).astype(jnp.bfloat16)]
  transfers between devices with their start and end apart: 7 -> 0, of which waited for: 6 -> 0; matrix products, arithmetic and copies ran while one was open for 9% -> 0% of each run, Pallas kernels for 0% -> 0%
where the time goes in v1:
time: 177 us
  Pallas kernels  165 us (93%)
  local copies, waits for them, and re-layouts  11.6 us (7%)
    pallas_call x1, Pallas kernels, on_device(): pl.pallas_call(body, out_shape=(jax.ShapeDtypeStruct((TOK, D), BF), jax.S...  165 us
    unnamed x6, local copies, waits for them, and re-layouts  10.1 us

profile of v1, /device:TPU:1, one launch (start us, length us, event | category | flops | bytes accessed | tf_op | source)
XLA Modules:
  0.0 177.1 jit_solution(15163512481521944804)
XLA Ops:
  0.6 1.4 copy.16.rw
  2.1 1.5 copy.15.ids
  3.5 164.9 %moe.1 = (bf16[256,2048]{1,0:T(8,128)(2,1)}, bf16[256,8]{1,0:T(8,128)(2,1)}, bf16[1,128,768]{2,1,0:T(8,128)(2,1)}, bf16[1,128,768]{2,1,0:T(8,128)(2,1)}, bf16[1,128,768]{2,1,0:T(8,128)(2,1)}) custom-call(bf16[256,2048]{1,0:T(8,128)(2,1)} %tok.1, bf16[256,2048]{1,0:T(8,128)(2,1)} %cot.1, s32[256,8]{1,0:T(8,128)} %copy.15.ids, bf16[256,8]{1,0:T(8,128)(2,1)} %copy.16.rw, ...), custom_call_target="tpu_custom_call" | custom-call | tf_op jit(solution)/shard_map/moe/pallas_call | solution.py:416
  168.4 1.5 copy.17
  169.9 2.3 %copy.22 = bf16[256,2048]{1,0:T(8,128)(2,1)} copy(bf16[256,2048]{1,0:T(8,128)(2,1)} %get-tuple-element.15) | data formatting | bytes 2097152
  172.2 1.6 copy.23
  173.8 1.6 copy.24
  175.4 1.6 copy.25

commit v2 on v1

v2 whole, which is shorter than its diff:
```python
import math

import jax
import jax.numpy as jnp
from jax import lax
from jax.experimental import pallas as pl
from jax.experimental.pallas import tpu as pltpu
from jax.sharding import PartitionSpec as P

MESH = pl.DeviceIdType.MESH
CAP = 24
LANES = 16
TOK = 256
D = 2048
FFN = 768
ROWS = LANES * CAP
PAIR = 2 * CAP
COLS = 256
CHUNKS = FFN // COLS
UNITS = 6 * CHUNKS
PAIRS = UNITS // 2
AHEAD = 3
DIRECT = (7, 8)
GROUPS = ((0, 3), (3, 3), (6, 2), (8, 1))
XBLK = D // 4
ZBLK = XBLK // 4
BF = jnp.bfloat16
F32 = jnp.float32
NT = (((1,), (1,)), ((), ()))


def iota(shape, dim):
    return lax.broadcasted_iota(jnp.int32, shape, dim)


def dot(a, b):
    return jnp.dot(a, b, preferred_element_type=F32)


def dot_nt(a, b):
    return lax.dot_general(a, b, NT, preferred_element_type=F32)


PLAN = (
    (),
    (("product", 0),),
    (("product", 1),),
    (("product", 2),),
    (("product", 3), ("step", 0, 1), ("step", 1, 1), ("step", 2, 1), ("combine",)),
    (("product", 4), ("step", 0, 2), ("step", 1, 2), ("step", 2, 2), ("step", 3, 1)),
    (("product", 5), ("last", 0), ("last", 1), ("last", 2), ("out", 0), ("step", 3, 2), ("step", 4, 1)),
    (("product", 6), ("last", 3), ("step", 4, 2), ("step", 5, 1)),
    (("product", 7), ("last", 4), ("step", 5, 2), ("step", 6, 1), ("pick", 0)),
    (("last", 5), ("out", 1), ("product", 8), ("step", 6, 2), ("last", 7), ("in", 0)),
    (("last", 6), ("out", 2), ("last", 8), ("out", 3)),
)


NEAR = (1, 2, 3, 4, 12, 5, 13, 6, 14, 7, 15, 8, 9, 10, 11)


def body(
    tok_h, cot_h, ids, rw, cap, old, old_s, new_s, wg_h, wu_h, wd_h,
    gx_h, gw, gg_h, gu_h, gd_h,
    tok, cot, wg, wu, wd, xs_send, xs_recv, xf, xb, sb, x4, s4, hb, ht, zb, zr,
    dx_send, dx_recv, ws_send, ws_recv, place_l, place_r, gx, gbuf, p1a, p1b, p1c, p1d, p2a, p2b, p2c, p2d, ob, go, wanted,
    w_sem, t_sem, o_sem, d_ss, d_rs, f_ss, f_rs, a_ss, a_rs, g_ss, g_rs, z_ss, z_rs,
    b_ss, b_rs, v_ss, v_rs, p_ss, p_rs, q_ss, q_rs,
):
    dp = lax.axis_index("dp")
    me = lax.axis_index("expert")
    x, zh = dp // 4, dp % 4
    y, zl, co = me // 4, (me // 2) % 2, me % 2
    p1, p2 = (p1a, p1b, p1c, p1d), (p2a, p2b, p2c, p2d)

    def at_x(s):
        return (((x + s + 4) % 4) * 4 + zh, me)

    def at_z(s):
        return (x * 4 + (zh + s + 4) % 4, me)

    def ahead(k):
        return ((y + k // 4) % 4) * 4 + ((zl + (k // 2) % 2) % 2) * 2 + (co + k % 2) % 2

    def behind(k):
        return ((y + 4 - k // 4) % 4) * 4 + ((zl + (k // 2) % 2) % 2) * 2 + (co + k % 2) % 2

    def remote(src, dst, ss, rs, device):
        return pltpu.make_async_remote_copy(
            src_ref=src, dst_ref=dst, send_sem=ss, recv_sem=rs,
            device_id=device, device_id_type=MESH,
        )

    def drain(ref, sem):
        pltpu.make_async_copy(ref, ref, sem).wait()

    rows_in = [
        pltpu.make_async_copy(h, v, t_sem.at[i])
        for i, (h, v) in enumerate(((tok_h, tok), (cot_h, cot)))
    ]
    weights = [
        pltpu.make_async_copy(h.at[0], v, w_sem.at[i])
        for i, (h, v) in enumerate(((wg_h, wg), (wu_h, wu), (wd_h, wd)))
    ]
    for copy in rows_in + weights:
        copy.start()
    barrier = pltpu.get_barrier_semaphore()
    for k in NEAR:
        pl.semaphore_signal(barrier, inc=1, device_id=(dp, ahead(k)), device_id_type=MESH)
    for s in (1, 2, 3):
        pl.semaphore_signal(barrier, inc=1, device_id=at_x(s), device_id_type=MESH)
    for s in (1, 2, 3):
        pl.semaphore_signal(barrier, inc=1, device_id=at_z(s), device_id_type=MESH)

    ids_t = ids[...].astype(F32)
    rw_t = rw[...].astype(F32)
    mine = old[...] == iota((LANES, LANES), 0)
    ex = jnp.sum(jnp.where(mine, iota((LANES, LANES), 1), 0).astype(F32), axis=1, keepdims=True)
    limit = jnp.sum(jnp.where(mine, cap[...], 0).astype(F32), axis=1, keepdims=True)
    named = jnp.zeros((LANES, TOK), F32)
    w_sel = jnp.zeros((LANES, TOK), F32)
    for k in range(8):
        hit = ids_t[k : k + 1, :] == ex
        named = named + jnp.where(hit, 1.0, 0.0)
        w_sel = w_sel + jnp.where(hit, rw_t[k : k + 1, :], 0.0)
    earlier = (iota((TOK, TOK), 0) < iota((TOK, TOK), 1)).astype(F32).astype(BF)
    before = dot(named.astype(BF), earlier)
    pos = jnp.where((named > 0.5) & (before < limit), before, -1.0)
    p_of = iota((CAP, TOK), 0).astype(F32)
    ones = [jnp.where(pos[s : s + 1, :] == p_of, 1.0, 0.0) for s in range(LANES)]
    place = jnp.concatenate(ones, axis=0).astype(BF)
    place_w = jnp.concatenate(
        [one * w_sel[s : s + 1, :] for s, one in enumerate(ones)], axis=0
    ).astype(BF)
    for copy in rows_in:
        copy.wait()
    for c in range(D // 256):
        cols = slice(256 * c, 256 * c + 256)
        rows_x = dot(place, tok[:, cols])
        rows_s = dot(place_w, cot[:, cols])
        both = []
        for s in range(LANES):
            both += [rows_x[CAP * s : CAP * s + CAP], rows_s[CAP * s : CAP * s + CAP]]
        xs_send[:, cols] = jnp.concatenate(both, axis=0).astype(BF)

    pl.semaphore_wait(barrier, LANES - 1 + 6)

    def block(k):
        return pl.ds(PAIR * k, PAIR)

    def dispatch(k):
        to = ahead(k)
        return remote(
            xs_send.at[pl.ds(pl.multiple_of(PAIR * to, 16), PAIR)], xs_recv.at[block(k)],
            d_ss, d_rs.at[k], (dp, to),
        )

    def columns(s):
        return pl.ds(pl.multiple_of(XBLK * ((x + s) % 4), XBLK), XBLK)

    def forward(k):
        for s in (2, 1, 3):
            remote(
                xs_recv.at[block(k), columns(s)], xf.at[s - 1, block(k)],
                f_ss, f_rs.at[s - 1], at_x(s),
            ).start()

    for k in NEAR:
        dispatch(k).start()
    xs_recv[0:PAIR] = xs_send[pl.ds(pl.multiple_of(PAIR * me, 16), PAIR)]
    forward(0)

    nothing = jnp.zeros((CAP, TOK), F32)
    left, right = [], []
    for one in ones:
        left += [one, nothing]
        right += [nothing, one]
    place_l[...] = jnp.concatenate(left, axis=0).astype(BF)
    place_r[...] = jnp.concatenate(right, axis=0).astype(BF)

    def look_up(j, carry):
        slot = jnp.int32(0)
        for n in range(LANES):
            slot = slot + jnp.where(new_s[n] == j, old_s[n], 0)
        wanted[j] = slot
        return carry

    lax.fori_loop(0, LANES, look_up, 0)
    for copy in weights:
        copy.wait()
    for k in NEAR:
        dispatch(k).wait_recv()
        forward(k)

    def split(src, cols):
        both = src[:, cols].astype(F32)
        return [
            jnp.concatenate(
                [both[PAIR * k + at : PAIR * k + at + CAP] for k in range(LANES)], axis=0
            ).astype(BF)
            for at in (0, CAP)
        ]

    for c in range(D // 256):
        cols = slice(256 * c, 256 * c + 256)
        xb[:, cols], sb[:, cols] = split(xs_recv, cols)

    def hidden_chunk(c, ws):
        cols = slice(COLS * c, COLS * c + COLS)
        gate = dot(xb[...], wg[:, cols])
        up = dot(xb[...], wu[:, cols])
        dh = dot(sb[...], wd[:, cols])
        sig = 1.0 / (1.0 + jnp.exp(-gate))
        act = gate * sig
        hidden = (act * up).astype(BF)
        dgate = dh * up * (sig * (1.0 + gate * (1.0 - sig)))
        dup = dh * act
        hb[0, :, cols] = dgate.astype(BF)
        hb[1, :, cols] = dup.astype(BF)
        hidden = hidden.astype(F32)
        for m, value in enumerate((dgate, dup, hidden)):
            turned = value.T.astype(BF)
            for h in range(2):
                ht[0, 6 * c + 2 * m + h] = turned[128 * h : 128 * h + 128]
        return ws + jnp.sum(hidden * dh, axis=1, keepdims=True)

    scale = 1.0 / math.sqrt(4 * 4 * LANES * CAP)

    def units_of(j):
        return (2 * j, 2 * j + 1)

    def sign(u):
        return 1 if u % 2 == 0 else -1

    def share(u, s):
        slot = 1 if s == 1 else 3
        return remote(ht.at[0, u], ht.at[slot, u], a_ss.at[slot // 2, u], a_rs.at[slot // 2, u], at_x(s))

    def pass_on(u):
        s = sign(u)
        return remote(ht.at[1 if s == 1 else 3, u], ht.at[2, u], g_ss.at[u], g_rs.at[u], at_x(s))

    def share_start(j):
        up, down = units_of(j)
        share(up, 1).start()
        share(down, -1).start()
        share(down, 1).start()
        share(up, -1).start()

    def share_pass(j):
        for u in units_of(j):
            share(u, sign(u)).wait_recv()
            pass_on(u).start()

    def share_rest(j):
        for u in units_of(j):
            share(u, -sign(u)).wait_recv()

    def z_block(u, k):
        return (zh - sign(u) * (1 + k) + 8) % 4

    def z_copy(u, k):
        return remote(
            zb.at[u, z_block(u, k)], zr.at[k, u], z_ss.at[k, u], z_rs.at[k, u], at_z(sign(u))
        )

    def z_direct(j, s):
        both = pl.ds(2 * j, 2)
        return remote(
            zb.at[both, (zh + s) % 4], zr.at[s - 1, both],
            z_ss.at[s - 1, 2 * j], z_rs.at[s - 1, 2 * j], at_z(s),
        )

    def product(j):
        rows = s4 if j % 3 == 2 else x4
        up, down = units_of(j)
        total = jnp.zeros((COLS, XBLK), F32)
        for s in (0, 1, 3, 2):
            if s == 2:
                for u in units_of(j):
                    pass_on(u).wait_recv()
            total = total + dot(ht[s, up : down + 1].reshape(COLS, ROWS), rows[s])
        total = (total * scale).astype(BF)
        for h, u in enumerate(units_of(j)):
            for q in range(4):
                zb[u, q] = total[128 * h : 128 * h + 128, ZBLK * q : ZBLK * q + ZBLK]
            if j not in DIRECT:
                z_copy(u, 0).start()
        if j in DIRECT:
            for s in (2, 1, 3):
                z_direct(j, s).start()
        for u in units_of(j):
            share(u, 1).wait_send()
            share(u, -1).wait_send()
            pass_on(u).wait_send()

    def z_step(j, k):
        for u in units_of(j):
            z_copy(u, k - 1).wait_recv()
            b = z_block(u, k)
            zb[u, b] = (zb[u, b].astype(F32) + zr[k - 1, u].astype(F32)).astype(BF)
            z_copy(u, k).start()
            z_copy(u, k - 1).wait_send()

    def z_last(j):
        if j in DIRECT:
            for s in (1, 3, 2):
                z_direct(j, s).wait_recv()
            for u in units_of(j):
                total = zb[u, zh].astype(F32)
                for s in range(3):
                    total = total + zr[s, u].astype(F32)
                gbuf[u] = total.T.astype(BF)
            for s in (1, 3, 2):
                z_direct(j, s).wait_send()
            return
        for u in units_of(j):
            z_copy(u, 2).wait_recv()
            total = zb[u, zh].astype(F32) + zr[2, u].astype(F32)
            gbuf[u] = total.T.astype(BF)
            z_copy(u, 2).wait_send()

    def piece(g, n):
        first, count = GROUPS[g]
        units = pl.ds(2 * first + count * (n % 2), count)
        return units, pl.ds(pl.multiple_of(16 * (n // 2), 16), 16)

    def move_out(g):
        for k in NEAR:
            to = ahead(k)
            remote(
                gbuf.at[*piece(g, to)], p1[g].at[me], p_ss.at[g], p_rs.at[g], (dp, to)
            ).start()
        p1[g][me] = gbuf[*piece(g, me)]

    def move_pick(g):
        drain(p1[g].at[0 : LANES - 1], p_rs.at[g])

        def pick(j, carry):
            p2[g][j] = p1[g][wanted[j]]
            return carry

        lax.fori_loop(0, LANES, pick, 0)
        for k in NEAR:
            to = ahead(k)
            remote(
                p2[g].at[to], ob.at[*piece(g, me)], q_ss.at[g], q_rs.at[g], (dp, to)
            ).start()
        ob[*piece(g, me)] = p2[g][me]
        drain(p1[g].at[0 : LANES - 1], p_ss.at[g])

    def result(j):
        cols = pl.ds(COLS * (j // 3), COLS)
        return pltpu.make_async_copy(
            go.at[j % 3, :, cols], (gg_h, gu_h, gd_h)[j % 3].at[0, :, cols], o_sem.at[1 + j]
        )

    def move_in(g):
        drain(p2[g].at[0 : LANES - 1], q_rs.at[g])
        first, count = GROUPS[g]
        for j in range(first, first + count):
            for h, u in enumerate(units_of(j)):
                at = COLS * (j // 3) + 128 * h
                go[j % 3, :, at : at + 128] = ob[u]
            result(j).start()
        drain(p2[g].at[0 : LANES - 1], q_ss.at[g])

    diagonal = iota((CAP, 128), 0) == iota((CAP, 128), 1)

    def send_back(ws):
        ws = ws / math.sqrt(D)
        for k in range(LANES):
            row = jnp.sum(
                jnp.where(diagonal, ws[CAP * k : CAP * k + CAP], 0.0), axis=0, keepdims=True
            )
            ws_send[k] = jnp.broadcast_to(row, (8, 128))
        for c in range(4):
            halves = []
            for half in range(2):
                at = 1024 * half + 256 * c
                halves.append(
                    dot_nt(hb[0], wg[at : at + 256, :]) + dot_nt(hb[1], wu[at : at + 256, :])
                )
            both = []
            for k in range(LANES):
                both += [part[CAP * k : CAP * k + CAP] for part in halves]
            dx_send[:, 256 * c : 256 * c + 256] = jnp.concatenate(both, axis=0).astype(BF)
        at_me = pl.ds(pl.multiple_of(PAIR * me, 16), PAIR)
        for k in NEAR:
            to = behind(k)
            remote(dx_send.at[block(k)], dx_recv.at[at_me], b_ss, b_rs, (dp, to)).start()
            remote(ws_send.at[k], ws_recv.at[me], v_ss, v_rs, (dp, to)).start()
        dx_recv[at_me] = dx_send[0:PAIR]
        ws_recv[me] = ws_send[0]

    gx_out = pltpu.make_async_copy(gx, gx_h, o_sem.at[0])

    def combine():
        drain(dx_send.at[0 : PAIR * (LANES - 1)], b_rs)
        drain(ws_send.at[0 : LANES - 1], v_rs)
        for half, table in enumerate((place_l, place_r)):
            turned = table[...].astype(F32).T.astype(BF)
            for c in range(2):
                at = 1024 * half + 512 * c
                gx[:, at : at + 512] = dot(turned, dx_recv[:, 512 * c : 512 * c + 512]).astype(BF)
        gx_out.start()
        chosen = []
        for s in range(LANES):
            column = jnp.sum(
                jnp.where(diagonal, ws_recv[s, 0:1, :], 0.0), axis=1, keepdims=True
            )
            one = place_l[PAIR * s : PAIR * s + PAIR].astype(F32)[0:CAP]
            chosen.append(jnp.sum(one * column, axis=0, keepdims=True))
        chosen = jnp.concatenate(chosen, axis=0)
        parts = [
            jnp.sum(jnp.where(ids_t[k : k + 1, :] == ex, chosen, 0.0), axis=0, keepdims=True)
            for k in range(8)
        ]
        gw[...] = (jnp.concatenate(parts, axis=0) / rw_t).astype(BF)
        drain(dx_send.at[0 : PAIR * (LANES - 1)], b_ss)
        drain(ws_send.at[0 : LANES - 1], v_ss)

    ws = hidden_chunk(0, jnp.zeros((ROWS, 1), F32))
    for j in range(AHEAD):
        share_start(j)
    ws = hidden_chunk(1, ws)
    ws = hidden_chunk(2, ws)
    send_back(ws)
    for s in range(4):
        if s == 0:
            own = pl.ds(pl.multiple_of(XBLK * x, XBLK), XBLK)
            x4[0], s4[0] = xb[:, own], sb[:, own]
        else:
            drain(xf.at[s - 1], f_rs.at[s - 1])
            x4[s], s4[s] = split(xf.at[s - 1], slice(None))
    drain(xs_send.at[0 : PAIR * (LANES - 1)], d_ss)
    drain(xf, f_ss)
    for j in range(PAIRS + 2):
        if j < PAIRS:
            share_pass(j)
        if j + AHEAD < PAIRS:
            share_start(j + AHEAD)
        if j < PAIRS:
            share_rest(j)
        for step, *args in PLAN[j]:
            {
                "product": product, "step": z_step, "last": z_last, "combine": combine,
                "out": move_out, "pick": move_pick, "in": move_in,
            }[step](*args)
    for g in range(1, 4):
        move_pick(g)
    for g in range(1, 4):
        move_in(g)
    gx_out.wait()
    for j in range(PAIRS):
        result(j).wait()


def hand_over(*refs):
    sources, results, held, sems = refs[:5], refs[5:10], refs[10:15], refs[15]
    arrive = [
        pltpu.make_async_copy(a, b, sems.at[0, i]) for i, (a, b) in enumerate(zip(sources, held))
    ]
    leave = [
        pltpu.make_async_copy(a, b, sems.at[1, i]) for i, (a, b) in enumerate(zip(held, results))
    ]
    for copy in arrive:
        copy.start()
    for before, after in zip(arrive, leave):
        before.wait()
        after.start()
    for copy in leave:
        copy.wait()


def on_device(
    tokens, cotangent, route_ids, route_weights, capacity, old_owner, new_owner, w_gate, w_up, w_down
):
    vmem = pl.BlockSpec(memory_space=pltpu.VMEM)
    smem = pl.BlockSpec(memory_space=pltpu.SMEM)
    hbm = pl.BlockSpec(memory_space=pl.ANY)
    dma = pltpu.SemaphoreType.DMA
    shard = jax.ShapeDtypeStruct((1, 128, FFN), BF)
    shapes = (
        jax.ShapeDtypeStruct((TOK, D), BF),
        jax.ShapeDtypeStruct((8, TOK), BF),
        shard, shard, shard,
    )
    V = pltpu.VMEM
    parts = pl.pallas_call(
        body,
        out_shape=shapes,
        in_specs=[hbm] * 2 + [vmem] * 4 + [smem] * 2 + [hbm] * 3,
        out_specs=[hbm, vmem, hbm, hbm, hbm],
        scratch_shapes=[
            V((TOK, D), BF), V((TOK, D), BF),
            V((D, FFN), BF), V((D, FFN), BF), V((D, FFN), BF),
            V((2 * ROWS, D), BF), V((2 * ROWS, D), BF), V((3, 2 * ROWS, XBLK), BF),
            V((ROWS, D), BF), V((ROWS, D), BF),
            V((4, ROWS, XBLK), BF), V((4, ROWS, XBLK), BF),
            V((2, ROWS, FFN), BF), V((4, UNITS, 128, ROWS), BF),
            V((UNITS, 4, 128, ZBLK), BF), V((3, UNITS, 128, ZBLK), BF),
            V((2 * ROWS, D // 2), BF), V((2 * ROWS, D // 2), BF),
            V((LANES, 8, 128), F32), V((LANES, 8, 128), F32),
            V((2 * ROWS, TOK), BF), V((2 * ROWS, TOK), BF),
            V((TOK, D), BF),
            V((UNITS, 128, 128), BF),
            *[V((LANES, count, 16, 128), BF) for _, count in GROUPS + GROUPS],
            V((UNITS, 128, 128), BF),
            V((3, 128, FFN), BF),
            pltpu.SMEM((LANES,), jnp.int32),
            dma((3,)), dma((2,)), dma((1 + PAIRS,)),
            dma, dma((LANES,)), dma, dma((3,)),
            dma((2, UNITS)), dma((2, UNITS)), dma((UNITS,)), dma((UNITS,)),
            dma((3, UNITS)), dma((3, UNITS)),
            dma, dma, dma, dma,
            dma((4,)), dma((4,)), dma((4,)), dma((4,)),
        ],
        compiler_params=pltpu.CompilerParams(
            collective_id=0, has_side_effects=True, vmem_limit_bytes=62 * 1024 * 1024
        ),
        name="moe",
    )(
        tokens, cotangent, route_ids.T, route_weights.T,
        capacity[None], old_owner[None], old_owner, new_owner,
        w_gate, w_up, w_down,
    )
    grad_x, grad_w, gate, up, down = pl.pallas_call(
        hand_over,
        out_shape=shapes,
        in_specs=[hbm] * 5,
        out_specs=[hbm] * 5,
        scratch_shapes=[V(held.shape, BF) for held in shapes] + [dma((2, 5))],
        compiler_params=pltpu.CompilerParams(vmem_limit_bytes=62 * 1024 * 1024),
        name="results",
    )(*parts)
    return grad_x, grad_w.T, gate, up, down


def solution(mesh):
    rows = P(("dp", "expert"), None)
    slots = P("expert", None, None)
    shards = P("expert", "dp", None)
    return jax.shard_map(
        on_device,
        mesh=mesh,
        in_specs=(rows, rows, rows, rows, P(), P(), P(), slots, slots, slots),
        out_specs=(rows, rows, shards, shards, shards),
        check_vma=False,
    )
```

time: 177 us -> 155 us (0.88)
  local copies, waits for them, and re-layouts: 11.6 us -> 0 us
  Pallas kernels: 165 us -> 154 us
    pallas_call x1 -> x2, Pallas kernels: 165 us -> 154 us  [the longest x1 152 us: on_device(): pl.pallas_call(body, out_shape=shapes, in_specs=[hbm] * 2 + [vmem] * 4 +...]
    unnamed x6 -> x0, local copies, waits for them, and re-layouts: 10.1 us -> none
where the time goes in v2:
time: 155 us
  Pallas kernels  154 us (99%)
    pallas_call x1, Pallas kernels, on_device(): pl.pallas_call(body, out_shape=shapes, in_specs=[hbm] * 2 + [vmem] * 4 +...  152 us

profile of v2, /device:TPU:1, one launch (start us, length us, event | category | flops | bytes accessed | tf_op | source)
XLA Modules:
  0.0 154.8 jit_solution(17102225266437702960)
XLA Ops:
  0.6 151.6 %moe.1 = (bf16[256,2048]{1,0:T(8,128)(2,1)}, bf16[8,256]{1,0:T(8,128)(2,1)}, bf16[1,128,768]{2,1,0:T(8,128)(2,1)}, bf16[1,128,768]{2,1,0:T(8,128)(2,1)}, bf16[1,128,768]{2,1,0:T(8,128)(2,1)}) custom-call(bf16[256,2048]{1,0:T(8,128)(2,1)} %tok_h.1, bf16[256,2048]{1,0:T(8,128)(2,1)} %cot_h.1, s32[8,256]{1,0:T(8,128)} %bitcast.5, bf16[8,256]{1,0:T(8,128)(2,1)} %bitcast.6, ...), custom_call_target="tpu_custom_call" | custom-call | tf_op jit(solution)/shard_map/moe/pallas_call | solution.py:490
  152.2 2.5 %results.1 = (bf16[256,2048]{1,0:T(8,128)(2,1)}, bf16[8,256]{1,0:T(8,128)(2,1)}, bf16[1,128,768]{2,1,0:T(8,128)(2,1)}, bf16[1,128,768]{2,1,0:T(8,128)(2,1)}, bf16[1,128,768]{2,1,0:T(8,128)(2,1)}) custom-call(bf16[256,2048]{1,0:T(8,128)(2,1)} %get-tuple-element.15.refs_0_, bf16[8,256]{1,0:T(8,128)(2,1)} %get-tuple-element.16.refs_1_, ...), custom_call_target="tpu_custom_call" | custom-call | tf_op jit(solution)/shard_map/results/pallas_call | solution.py:528

commit v3 on v2

--- a/solution.py
+++ b/solution.py
@@ -20,8 +20,7 @@
 UNITS = 6 * CHUNKS
 PAIRS = UNITS // 2
 AHEAD = 3
-DIRECT = (7, 8)
-GROUPS = ((0, 3), (3, 3), (6, 2), (8, 1))
+GROUPS = ((0, 4), (4, 3), (7, 2))
 XBLK = D // 4
 ZBLK = XBLK // 4
 BF = jnp.bfloat16
@@ -45,45 +44,48 @@
     (),
     (("product", 0),),
     (("product", 1),),
-    (("product", 2),),
-    (("product", 3), ("step", 0, 1), ("step", 1, 1), ("step", 2, 1), ("combine",)),
-    (("product", 4), ("step", 0, 2), ("step", 1, 2), ("step", 2, 2), ("step", 3, 1)),
-    (("product", 5), ("last", 0), ("last", 1), ("last", 2), ("out", 0), ("step", 3, 2), ("step", 4, 1)),
-    (("product", 6), ("last", 3), ("step", 4, 2), ("step", 5, 1)),
-    (("product", 7), ("last", 4), ("step", 5, 2), ("step", 6, 1), ("pick", 0)),
-    (("last", 5), ("out", 1), ("product", 8), ("step", 6, 2), ("last", 7), ("in", 0)),
-    (("last", 6), ("out", 2), ("last", 8), ("out", 3)),
+    (("product", 2), ("last", 0), ("combine",)),
+    (("product", 3), ("last", 1)),
+    (("product", 4), ("last", 2)),
+    (("product", 5), ("last", 3), ("out", 0)),
+    (("product", 6), ("last", 4), ("pick", 0)),
+    (("product", 7), ("product", 8), ("last", 5), ("in", 0)),
+    (
+        ("last", 6), ("out", 1), ("last", 7), ("last", 8), ("out", 2),
+        ("pick", 1), ("pick", 2), ("in", 1), ("in", 2),
+    ),
 )
 
 
 NEAR = (1, 2, 3, 4, 12, 5, 13, 6, 14, 7, 15, 8, 9, 10, 11)
+HALF = ROWS // 2
 
 
 def body(
     tok_h, cot_h, ids, rw, cap, old, old_s, new_s, wg_h, wu_h, wd_h,
     gx_h, gw, gg_h, gu_h, gd_h,
     tok, cot, wg, wu, wd, xs_send, xs_recv, xf, xb, sb, x4, s4, hb, ht, zb, zr,
-    dx_send, dx_recv, ws_send, ws_recv, place_l, place_r, gx, gbuf, p1a, p1b, p1c, p1d, p2a, p2b, p2c, p2d, ob, go, wanted,
+    dx_send, dx_recv, ws_send, ws_recv, place_l, place_r, gx, gbuf, ob, go, wanted,
     w_sem, t_sem, o_sem, d_ss, d_rs, f_ss, f_rs, a_ss, a_rs, g_ss, g_rs, z_ss, z_rs,
-    b_ss, b_rs, v_ss, v_rs, p_ss, p_rs, q_ss, q_rs,
+    b_ss, b_rs, v_ss, v_rs, p_ss, p_rs, q_ss, q_rs, *moved,
 ):
     dp = lax.axis_index("dp")
     me = lax.axis_index("expert")
-    x, zh = dp // 4, dp % 4
-    y, zl, co = me // 4, (me // 2) % 2, me % 2
-    p1, p2 = (p1a, p1b, p1c, p1d), (p2a, p2b, p2c, p2d)
+    x, zh = lax.div(dp, 4), lax.rem(dp, 4)
+    y, zl, co = lax.div(me, 4), lax.rem(lax.div(me, 2), 2), lax.rem(me, 2)
+    p1, p2 = moved[: len(GROUPS)], moved[len(GROUPS) :]
 
     def at_x(s):
-        return (((x + s + 4) % 4) * 4 + zh, me)
+        return (lax.rem(x + (s + 4) % 4, 4) * 4 + zh, me)
 
     def at_z(s):
-        return (x * 4 + (zh + s + 4) % 4, me)
+        return (x * 4 + lax.rem(zh + (s + 4) % 4, 4), me)
 
     def ahead(k):
-        return ((y + k // 4) % 4) * 4 + ((zl + (k // 2) % 2) % 2) * 2 + (co + k % 2) % 2
+        return lax.rem(y + k // 4, 4) * 4 + lax.rem(zl + (k // 2) % 2, 2) * 2 + lax.rem(co + k % 2, 2)
 
     def behind(k):
-        return ((y + 4 - k // 4) % 4) * 4 + ((zl + (k // 2) % 2) % 2) * 2 + (co + k % 2) % 2
+        return lax.rem(y + 4 - k // 4, 4) * 4 + lax.rem(zl + (k // 2) % 2, 2) * 2 + lax.rem(co + k % 2, 2)
 
     def remote(src, dst, ss, rs, device):
         return pltpu.make_async_remote_copy(
@@ -145,8 +147,11 @@
 
     pl.semaphore_wait(barrier, LANES - 1 + 6)
 
+    def place_of(k):
+        return ((0,) + NEAR).index(k)
+
     def block(k):
-        return pl.ds(PAIR * k, PAIR)
+        return pl.ds(PAIR * place_of(k), PAIR)
 
     def dispatch(k):
         to = ahead(k)
@@ -156,7 +161,7 @@
         )
 
     def columns(s):
-        return pl.ds(pl.multiple_of(XBLK * ((x + s) % 4), XBLK), XBLK)
+        return pl.ds(pl.multiple_of(XBLK * lax.rem(x + s, 4), XBLK), XBLK)
 
     def forward(k):
         for s in (2, 1, 3):
@@ -188,41 +193,40 @@
     lax.fori_loop(0, LANES, look_up, 0)
     for copy in weights:
         copy.wait()
-    for k in NEAR:
-        dispatch(k).wait_recv()
-        forward(k)
-
-    def split(src, cols):
-        both = src[:, cols].astype(F32)
+    def split(src, cols, first=0, count=LANES):
+        both = src[PAIR * first : PAIR * (first + count), cols].astype(F32)
         return [
             jnp.concatenate(
-                [both[PAIR * k + at : PAIR * k + at + CAP] for k in range(LANES)], axis=0
+                [both[PAIR * k + at : PAIR * k + at + CAP] for k in range(count)], axis=0
             ).astype(BF)
             for at in (0, CAP)
         ]
 
-    for c in range(D // 256):
-        cols = slice(256 * c, 256 * c + 256)
-        xb[:, cols], sb[:, cols] = split(xs_recv, cols)
-
-    def hidden_chunk(c, ws):
+    def unpack(half):
+        rows = slice(HALF * half, HALF * half + HALF)
+        for c in range(D // 256):
+            cols = slice(256 * c, 256 * c + 256)
+            xb[rows, cols], sb[rows, cols] = split(xs_recv, cols, LANES // 2 * half, LANES // 2)
+
+    def hidden_chunk(half, c):
+        rows = slice(HALF * half, HALF * half + HALF)
         cols = slice(COLS * c, COLS * c + COLS)
-        gate = dot(xb[...], wg[:, cols])
-        up = dot(xb[...], wu[:, cols])
-        dh = dot(sb[...], wd[:, cols])
+        gate = dot(xb[rows], wg[:, cols])
+        up = dot(xb[rows], wu[:, cols])
+        dh = dot(sb[rows], wd[:, cols])
         sig = 1.0 / (1.0 + jnp.exp(-gate))
         act = gate * sig
         hidden = (act * up).astype(BF)
-        dgate = dh * up * (sig * (1.0 + gate * (1.0 - sig)))
-        dup = dh * act
-        hb[0, :, cols] = dgate.astype(BF)
-        hb[1, :, cols] = dup.astype(BF)
-        hidden = hidden.astype(F32)
-        for m, value in enumerate((dgate, dup, hidden)):
-            turned = value.T.astype(BF)
+        hb[0, rows, cols] = (dh * up * (sig * (1.0 + gate * (1.0 - sig)))).astype(BF)
+        hb[1, rows, cols] = (dh * act).astype(BF)
+        hb[2, rows, cols] = hidden
+        return jnp.sum(hidden.astype(F32) * dh, axis=1, keepdims=True)
+
+    def turn(c):
+        for m in range(3):
+            turned = hb[m, :, COLS * c : COLS * c + COLS].astype(F32).T.astype(BF)
             for h in range(2):
                 ht[0, 6 * c + 2 * m + h] = turned[128 * h : 128 * h + 128]
-        return ws + jnp.sum(hidden * dh, axis=1, keepdims=True)
 
     scale = 1.0 / math.sqrt(4 * 4 * LANES * CAP)
 
@@ -256,19 +260,11 @@
         for u in units_of(j):
             share(u, -sign(u)).wait_recv()
 
-    def z_block(u, k):
-        return (zh - sign(u) * (1 + k) + 8) % 4
-
-    def z_copy(u, k):
-        return remote(
-            zb.at[u, z_block(u, k)], zr.at[k, u], z_ss.at[k, u], z_rs.at[k, u], at_z(sign(u))
-        )
-
-    def z_direct(j, s):
+    def z_copy(j, s):
         both = pl.ds(2 * j, 2)
         return remote(
-            zb.at[both, (zh + s) % 4], zr.at[s - 1, both],
-            z_ss.at[s - 1, 2 * j], z_rs.at[s - 1, 2 * j], at_z(s),
+            zb.at[both, lax.rem(zh + s, 4)], zr.at[s - 1, both],
+            z_ss.at[s - 1, j], z_rs.at[s - 1, j], at_z(s),
         )
 
     def product(j):
@@ -284,53 +280,38 @@
         for h, u in enumerate(units_of(j)):
             for q in range(4):
                 zb[u, q] = total[128 * h : 128 * h + 128, ZBLK * q : ZBLK * q + ZBLK]
-            if j not in DIRECT:
-                z_copy(u, 0).start()
-        if j in DIRECT:
-            for s in (2, 1, 3):
-                z_direct(j, s).start()
+        for s in (2, 1, 3):
+            z_copy(j, s).start()
         for u in units_of(j):
             share(u, 1).wait_send()
             share(u, -1).wait_send()
             pass_on(u).wait_send()
 
-    def z_step(j, k):
+    def z_last(j):
+        for s in (1, 3, 2):
+            z_copy(j, s).wait_recv()
         for u in units_of(j):
-            z_copy(u, k - 1).wait_recv()
-            b = z_block(u, k)
-            zb[u, b] = (zb[u, b].astype(F32) + zr[k - 1, u].astype(F32)).astype(BF)
-            z_copy(u, k).start()
-            z_copy(u, k - 1).wait_send()
-
-    def z_last(j):
-        if j in DIRECT:
-            for s in (1, 3, 2):
-                z_direct(j, s).wait_recv()
-            for u in units_of(j):
-                total = zb[u, zh].astype(F32)
-                for s in range(3):
-                    total = total + zr[s, u].astype(F32)
-                gbuf[u] = total.T.astype(BF)
-            for s in (1, 3, 2):
-                z_direct(j, s).wait_send()
-            return
-        for u in units_of(j):
-            z_copy(u, 2).wait_recv()
-            total = zb[u, zh].astype(F32) + zr[2, u].astype(F32)
+            total = zb[u, zh].astype(F32)
+            for s in range(3):
+                total = total + zr[s, u].astype(F32)
             gbuf[u] = total.T.astype(BF)
-            z_copy(u, 2).wait_send()
+        for s in (1, 3, 2):
+            z_copy(j, s).wait_send()
 
     def piece(g, n):
         first, count = GROUPS[g]
-        units = pl.ds(2 * first + count * (n % 2), count)
-        return units, pl.ds(pl.multiple_of(16 * (n // 2), 16), 16)
+        units = pl.ds(2 * first + count * lax.rem(n, 2), count)
+        return units, pl.ds(pl.multiple_of(16 * lax.div(n, 2), 16), 16)
 
     def move_out(g):
-        for k in NEAR:
-            to = ahead(k)
-            remote(
-                gbuf.at[*piece(g, to)], p1[g].at[me], p_ss.at[g], p_rs.at[g], (dp, to)
-            ).start()
+        first, count = GROUPS[g]
+        for n in range(LANES):
+
+            @pl.when(n != me)
+            def _(n=n):
+                at = 2 * first + count * (n % 2)
+                part = gbuf.at[at : at + count, 16 * (n // 2) : 16 * (n // 2) + 16]
+                remote(part, p1[g].at[me], p_ss.at[g], p_rs.at[g], (dp, n)).start()
         p1[g][me] = gbuf[*piece(g, me)]
 
     def move_pick(g):
@@ -341,11 +322,12 @@
             return carry
 
         lax.fori_loop(0, LANES, pick, 0)
-        for k in NEAR:
-            to = ahead(k)
-            remote(
-                p2[g].at[to], ob.at[*piece(g, me)], q_ss.at[g], q_rs.at[g], (dp, to)
-            ).start()
+        here = ob.at[*piece(g, me)]
+        for n in range(LANES):
+
+            @pl.when(n != me)
+            def _(n=n):
+                remote(p2[g].at[n], here, q_ss.at[g], q_rs.at[g], (dp, n)).start()
         ob[*piece(g, me)] = p2[g][me]
         drain(p1[g].at[0 : LANES - 1], p_ss.at[g])
 
@@ -367,31 +349,40 @@
 
     diagonal = iota((CAP, 128), 0) == iota((CAP, 128), 1)
 
-    def send_back(ws):
+    def back_rows(half, ws):
         ws = ws / math.sqrt(D)
-        for k in range(LANES):
+        rows = slice(HALF * half, HALF * half + HALF)
+        for k in range(LANES // 2):
             row = jnp.sum(
                 jnp.where(diagonal, ws[CAP * k : CAP * k + CAP], 0.0), axis=0, keepdims=True
             )
-            ws_send[k] = jnp.broadcast_to(row, (8, 128))
+            ws_send[LANES // 2 * half + k] = jnp.broadcast_to(row, (8, 128))
         for c in range(4):
-            halves = []
-            for half in range(2):
-                at = 1024 * half + 256 * c
-                halves.append(
-                    dot_nt(hb[0], wg[at : at + 256, :]) + dot_nt(hb[1], wu[at : at + 256, :])
+            sides = []
+            for side in range(2):
+                at = 1024 * side + 256 * c
+                sides.append(
+                    dot_nt(hb[0, rows], wg[at : at + 256, :])
+                    + dot_nt(hb[1, rows], wu[at : at + 256, :])
                 )
             both = []
-            for k in range(LANES):
-                both += [part[CAP * k : CAP * k + CAP] for part in halves]
-            dx_send[:, 256 * c : 256 * c + 256] = jnp.concatenate(both, axis=0).astype(BF)
+            for k in range(LANES // 2):
+                both += [part[CAP * k : CAP * k + CAP] for part in sides]
+            dx_send[2 * HALF * half : 2 * HALF * (half + 1), 256 * c : 256 * c + 256] = (
+                jnp.concatenate(both, axis=0).astype(BF)
+            )
+
+    def back_start(half):
         at_me = pl.ds(pl.multiple_of(PAIR * me, 16), PAIR)
         for k in NEAR:
+            if place_of(k) // (LANES // 2) != half:
+                continue
             to = behind(k)
             remote(dx_send.at[block(k)], dx_recv.at[at_me], b_ss, b_rs, (dp, to)).start()
-            remote(ws_send.at[k], ws_recv.at[me], v_ss, v_rs, (dp, to)).start()
-        dx_recv[at_me] = dx_send[0:PAIR]
-        ws_recv[me] = ws_send[0]
+            remote(ws_send.at[place_of(k)], ws_recv.at[me], v_ss, v_rs, (dp, to)).start()
+        if half == 0:
+            dx_recv[at_me] = dx_send[0:PAIR]
+            ws_recv[me] = ws_send[0]
 
     gx_out = pltpu.make_async_copy(gx, gx_h, o_sem.at[0])
 
@@ -420,12 +411,27 @@
         drain(dx_send.at[0 : PAIR * (LANES - 1)], b_ss)
         drain(ws_send.at[0 : LANES - 1], v_ss)
 
-    ws = hidden_chunk(0, jnp.zeros((ROWS, 1), F32))
+    value = jnp.zeros((HALF, 1), F32)
+    for i, k in enumerate(NEAR):
+        dispatch(k).wait_recv()
+        forward(k)
+        if i == LANES // 2 - 2:
+            unpack(0)
+        if 0 <= i - LANES // 2 + 1 < CHUNKS:
+            value = value + hidden_chunk(0, i - LANES // 2 + 1)
+        if i == LANES // 2 - 1 + CHUNKS:
+            back_rows(0, value)
+    back_start(0)
+    unpack(1)
+    value = hidden_chunk(1, 0)
+    turn(0)
     for j in range(AHEAD):
         share_start(j)
-    ws = hidden_chunk(1, ws)
-    ws = hidden_chunk(2, ws)
-    send_back(ws)
+    for c in range(1, CHUNKS):
+        value = value + hidden_chunk(1, c)
+        turn(c)
+    back_rows(1, value)
+    back_start(1)
     for s in range(4):
         if s == 0:
             own = pl.ds(pl.multiple_of(XBLK * x, XBLK), XBLK)
@@ -435,22 +441,18 @@
             x4[s], s4[s] = split(xf.at[s - 1], slice(None))
     drain(xs_send.at[0 : PAIR * (LANES - 1)], d_ss)
     drain(xf, f_ss)
-    for j in range(PAIRS + 2):
+    for j in range(len(PLAN)):
         if j < PAIRS:
             share_pass(j)
-        if j + AHEAD < PAIRS:
-            share_start(j + AHEAD)
+        if 0 < j < PAIRS - AHEAD + 1:
+            share_start(j + AHEAD - 1)
         if j < PAIRS:
             share_rest(j)
         for step, *args in PLAN[j]:
             {
-                "product": product, "step": z_step, "last": z_last, "combine": combine,
-                "out": move_out, "pick": move_pick, "in": move_in,
+                "product": product, "last": z_last, "combine": combine, "out": move_out,
+                "pick": move_pick, "in": move_in,
             }[step](*args)
-    for g in range(1, 4):
-        move_pick(g)
-    for g in range(1, 4):
-        move_in(g)
     gx_out.wait()
     for j in range(PAIRS):
         result(j).wait()
@@ -498,23 +500,23 @@
             V((2 * ROWS, D), BF), V((2 * ROWS, D), BF), V((3, 2 * ROWS, XBLK), BF),
             V((ROWS, D), BF), V((ROWS, D), BF),
             V((4, ROWS, XBLK), BF), V((4, ROWS, XBLK), BF),
-            V((2, ROWS, FFN), BF), V((4, UNITS, 128, ROWS), BF),
+            V((3, ROWS, FFN), BF), V((4, UNITS, 128, ROWS), BF),
             V((UNITS, 4, 128, ZBLK), BF), V((3, UNITS, 128, ZBLK), BF),
             V((2 * ROWS, D // 2), BF), V((2 * ROWS, D // 2), BF),
             V((LANES, 8, 128), F32), V((LANES, 8, 128), F32),
             V((2 * ROWS, TOK), BF), V((2 * ROWS, TOK), BF),
             V((TOK, D), BF),
             V((UNITS, 128, 128), BF),
-            *[V((LANES, count, 16, 128), BF) for _, count in GROUPS + GROUPS],
             V((UNITS, 128, 128), BF),
             V((3, 128, FFN), BF),
             pltpu.SMEM((LANES,), jnp.int32),
             dma((3,)), dma((2,)), dma((1 + PAIRS,)),
             dma, dma((LANES,)), dma, dma((3,)),
             dma((2, UNITS)), dma((2, UNITS)), dma((UNITS,)), dma((UNITS,)),
-            dma((3, UNITS)), dma((3, UNITS)),
+            dma((3, PAIRS)), dma((3, PAIRS)),
             dma, dma, dma, dma,
-            dma((4,)), dma((4,)), dma((4,)), dma((4,)),
+            *[dma((len(GROUPS),))] * 4,
+            *[V((LANES, count, 16, 128), BF) for _, count in GROUPS + GROUPS],
         ],
         compiler_params=pltpu.CompilerParams(
             collective_id=0, has_side_effects=True, vmem_limit_bytes=62 * 1024 * 1024

time: 155 us -> 146 us (0.942)
  Pallas kernels: 154 us -> 145 us
    pallas_call x1, Pallas kernels: 152 us -> 143 us  [on_device(): pl.pallas_call(body, out_shape=shapes, in_specs=[hbm] * 2 + [vmem] * 4 +...]
where the time goes in v3:
time: 146 us
  Pallas kernels  145 us (99%)
    pallas_call x1, Pallas kernels, on_device(): pl.pallas_call(body, out_shape=shapes, in_specs=[hbm] * 2 + [vmem] * 4 +...  143 us

profile of v3, /device:TPU:1, one launch (start us, length us, event | category | flops | bytes accessed | tf_op | source)
XLA Modules:
  0.0 146.2 jit_solution(9932047701858502993)
XLA Ops:
  0.6 142.9 %moe.1 = (bf16[256,2048]{1,0:T(8,128)(2,1)}, bf16[8,256]{1,0:T(8,128)(2,1)}, bf16[1,128,768]{2,1,0:T(8,128)(2,1)}, bf16[1,128,768]{2,1,0:T(8,128)(2,1)}, bf16[1,128,768]{2,1,0:T(8,128)(2,1)}) custom-call(bf16[256,2048]{1,0:T(8,128)(2,1)} %tok_h.1, bf16[256,2048]{1,0:T(8,128)(2,1)} %cot_h.1, s32[8,256]{1,0:T(8,128)} %bitcast.5, bf16[8,256]{1,0:T(8,128)(2,1)} %bitcast.6, ...), custom_call_target="tpu_custom_call" | custom-call | tf_op jit(solution)/shard_map/moe/pallas_call | solution.py:492
  143.6 2.5 %results.1 = (bf16[256,2048]{1,0:T(8,128)(2,1)}, bf16[8,256]{1,0:T(8,128)(2,1)}, bf16[1,128,768]{2,1,0:T(8,128)(2,1)}, bf16[1,128,768]{2,1,0:T(8,128)(2,1)}, bf16[1,128,768]{2,1,0:T(8,128)(2,1)}) custom-call(bf16[256,2048]{1,0:T(8,128)(2,1)} %get-tuple-element.15.refs_0_, bf16[8,256]{1,0:T(8,128)(2,1)} %get-tuple-element.16.refs_1_, ...), custom_call_target="tpu_custom_call" | custom-call | tf_op jit(solution)/shard_map/results/pallas_call | solution.py:530

commit v4 on v3

--- a/solution.py
+++ b/solution.py
@@ -63,9 +63,9 @@
 
 def body(
     tok_h, cot_h, ids, rw, cap, old, old_s, new_s, wg_h, wu_h, wd_h,
-    gx_h, gw, gg_h, gu_h, gd_h,
+    gx_h, gw_h, gg_h, gu_h, gd_h,
     tok, cot, wg, wu, wd, xs_send, xs_recv, xf, xb, sb, x4, s4, hb, ht, zb, zr,
-    dx_send, dx_recv, ws_send, ws_recv, place_l, place_r, gx, gbuf, ob, go, wanted,
+    dx_send, dx_recv, ws_send, ws_recv, place_l, place_r, gx, gw, gbuf, ob, go, wanted,
     w_sem, t_sem, o_sem, d_ss, d_rs, f_ss, f_rs, a_ss, a_rs, g_ss, g_rs, z_ss, z_rs,
     b_ss, b_rs, v_ss, v_rs, p_ss, p_rs, q_ss, q_rs, *moved,
 ):
@@ -334,7 +334,7 @@
     def result(j):
         cols = pl.ds(COLS * (j // 3), COLS)
         return pltpu.make_async_copy(
-            go.at[j % 3, :, cols], (gg_h, gu_h, gd_h)[j % 3].at[0, :, cols], o_sem.at[1 + j]
+            go.at[j % 3, :, cols], (gg_h, gu_h, gd_h)[j % 3].at[0, :, cols], o_sem.at[2 + j]
         )
 
     def move_in(g):
@@ -385,6 +385,7 @@
             ws_recv[me] = ws_send[0]
 
     gx_out = pltpu.make_async_copy(gx, gx_h, o_sem.at[0])
+    gw_out = pltpu.make_async_copy(gw, gw_h, o_sem.at[1])
 
     def combine():
         drain(dx_send.at[0 : PAIR * (LANES - 1)], b_rs)
@@ -408,6 +409,7 @@
             for k in range(8)
         ]
         gw[...] = (jnp.concatenate(parts, axis=0) / rw_t).astype(BF)
+        gw_out.start()
         drain(dx_send.at[0 : PAIR * (LANES - 1)], b_ss)
         drain(ws_send.at[0 : LANES - 1], v_ss)
 
@@ -454,6 +456,7 @@
                 "pick": move_pick, "in": move_in,
             }[step](*args)
     gx_out.wait()
+    gw_out.wait()
     for j in range(PAIRS):
         result(j).wait()
 
@@ -493,7 +496,7 @@
         body,
         out_shape=shapes,
         in_specs=[hbm] * 2 + [vmem] * 4 + [smem] * 2 + [hbm] * 3,
-        out_specs=[hbm, vmem, hbm, hbm, hbm],
+        out_specs=[hbm] * 5,
         scratch_shapes=[
             V((TOK, D), BF), V((TOK, D), BF),
             V((D, FFN), BF), V((D, FFN), BF), V((D, FFN), BF),
@@ -505,12 +508,12 @@
             V((2 * ROWS, D // 2), BF), V((2 * ROWS, D // 2), BF),
             V((LANES, 8, 128), F32), V((LANES, 8, 128), F32),
             V((2 * ROWS, TOK), BF), V((2 * ROWS, TOK), BF),
-            V((TOK, D), BF),
+            V((TOK, D), BF), V((8, TOK), BF),
             V((UNITS, 128, 128), BF),
             V((UNITS, 128, 128), BF),
             V((3, 128, FFN), BF),
             pltpu.SMEM((LANES,), jnp.int32),
-            dma((3,)), dma((2,)), dma((1 + PAIRS,)),
+            dma((3,)), dma((2,)), dma((2 + PAIRS,)),
             dma, dma((LANES,)), dma, dma((3,)),
             dma((2, UNITS)), dma((2, UNITS)), dma((UNITS,)), dma((UNITS,)),
             dma((3, PAIRS)), dma((3, PAIRS)),

time: 146 us -> 145 us (level)
  no operation moved by 1% of the time
where the time goes in v4:
time: 145 us
  Pallas kernels  144 us (99%)
    pallas_call x1, Pallas kernels, on_device(): pl.pallas_call(body, out_shape=shapes, in_specs=[hbm] * 2 + [vmem] * 4 +...  142 us

profile of v4, /device:TPU:1, one launch (start us, length us, event | category | flops | bytes accessed | tf_op | source)
XLA Modules:
  0.0 144.8 jit_solution(839449349839080870)
XLA Ops:
  0.6 141.5 %moe.1 = (bf16[256,2048]{1,0:T(8,128)(2,1)}, bf16[8,256]{1,0:T(8,128)(2,1)}, bf16[1,128,768]{2,1,0:T(8,128)(2,1)}, bf16[1,128,768]{2,1,0:T(8,128)(2,1)}, bf16[1,128,768]{2,1,0:T(8,128)(2,1)}) custom-call(bf16[256,2048]{1,0:T(8,128)(2,1)} %tok_h.1, bf16[256,2048]{1,0:T(8,128)(2,1)} %cot_h.1, s32[8,256]{1,0:T(8,128)} %bitcast.5, bf16[8,256]{1,0:T(8,128)(2,1)} %bitcast.6, ...), custom_call_target="tpu_custom_call" | custom-call | tf_op jit(solution)/shard_map/moe/pallas_call | solution.py:495
  142.2 2.5 %results.1 = (bf16[256,2048]{1,0:T(8,128)(2,1)}, bf16[8,256]{1,0:T(8,128)(2,1)}, bf16[1,128,768]{2,1,0:T(8,128)(2,1)}, bf16[1,128,768]{2,1,0:T(8,128)(2,1)}, bf16[1,128,768]{2,1,0:T(8,128)(2,1)}) custom-call(bf16[256,2048]{1,0:T(8,128)(2,1)} %get-tuple-element.15.refs_0_, bf16[8,256]{1,0:T(8,128)(2,1)} %get-tuple-element.16.refs_1_, ...), custom_call_target="tpu_custom_call" | custom-call | tf_op jit(solution)/shard_map/results/pallas_call | solution.py:533

commit v5 on v4

--- a/solution.py
+++ b/solution.py
@@ -20,7 +20,7 @@
 UNITS = 6 * CHUNKS
 PAIRS = UNITS // 2
 AHEAD = 3
-GROUPS = ((0, 4), (4, 3), (7, 2))
+GROUPS = ((0, 6), (6, 3))
 XBLK = D // 4
 ZBLK = XBLK // 4
 BF = jnp.bfloat16
@@ -47,12 +47,12 @@
     (("product", 2), ("last", 0), ("combine",)),
     (("product", 3), ("last", 1)),
     (("product", 4), ("last", 2)),
-    (("product", 5), ("last", 3), ("out", 0)),
-    (("product", 6), ("last", 4), ("pick", 0)),
-    (("product", 7), ("product", 8), ("last", 5), ("in", 0)),
+    (("product", 5), ("last", 3)),
+    (("product", 6), ("last", 4)),
+    (("product", 7), ("product", 8), ("last", 5), ("out", 0)),
     (
-        ("last", 6), ("out", 1), ("last", 7), ("last", 8), ("out", 2),
-        ("pick", 1), ("pick", 2), ("in", 1), ("in", 2),
+        ("last", 6), ("last", 7), ("last", 8), ("out", 1),
+        ("pick", 0), ("pick", 1), ("in", 0), ("in", 1),
     ),
 )
 

time: 145 us -> 144 us (level)
  no operation moved by 1% of the time
where the time goes in v5:
time: 144 us
  Pallas kernels  143 us (99%)
    pallas_call x1, Pallas kernels, on_device(): pl.pallas_call(body, out_shape=shapes, in_specs=[hbm] * 2 + [vmem] * 4 +...  141 us

profile of v5, /device:TPU:1, one launch (start us, length us, event | category | flops | bytes accessed | tf_op | source)
XLA Modules:
  0.0 143.7 jit_solution(8294730871940635285)
XLA Ops:
  0.6 140.5 %moe.1 = (bf16[256,2048]{1,0:T(8,128)(2,1)}, bf16[8,256]{1,0:T(8,128)(2,1)}, bf16[1,128,768]{2,1,0:T(8,128)(2,1)}, bf16[1,128,768]{2,1,0:T(8,128)(2,1)}, bf16[1,128,768]{2,1,0:T(8,128)(2,1)}) custom-call(bf16[256,2048]{1,0:T(8,128)(2,1)} %tok_h.1, bf16[256,2048]{1,0:T(8,128)(2,1)} %cot_h.1, s32[8,256]{1,0:T(8,128)} %bitcast.5, bf16[8,256]{1,0:T(8,128)(2,1)} %bitcast.6, ...), custom_call_target="tpu_custom_call" | custom-call | tf_op jit(solution)/shard_map/moe/pallas_call | solution.py:495
  141.2 2.5 %results.1 = (bf16[256,2048]{1,0:T(8,128)(2,1)}, bf16[8,256]{1,0:T(8,128)(2,1)}, bf16[1,128,768]{2,1,0:T(8,128)(2,1)}, bf16[1,128,768]{2,1,0:T(8,128)(2,1)}, bf16[1,128,768]{2,1,0:T(8,128)(2,1)}) custom-call(bf16[256,2048]{1,0:T(8,128)(2,1)} %get-tuple-element.15.refs_0_, bf16[8,256]{1,0:T(8,128)(2,1)} %get-tuple-element.16.refs_1_, ...), custom_call_target="tpu_custom_call" | custom-call | tf_op jit(solution)/shard_map/results/pallas_call | solution.py:533
